TPU v7x, 768 devices: a whole 4x8x12 slice. The times are simulated.
768 devices in a mesh: batch: 48 (over x, z), segment: 2 (over y_lo), seq: 8 (over y_hi, core).
Axes of the slice: x: 4, y: 8 (y_hi: 4, y_lo: 2; y = y_hi * 2 + y_lo), z: 12, core: 2. Of those that a mesh axis runs over, the one named last changes fastest.
Arguments:
- dna_features: bfloat16 [48, 2, 1536, 768], P('batch', None, 'seq'), may hold values from -6 to 6
- depth_weight: bfloat16 [3, 768], replicated, may hold values from -3.5 to 3.5
- point_weight: bfloat16 [768, 1536], replicated, may hold values from -0.21875 to 0.21875
- query_weight: bfloat16 [1536, 512], replicated, may hold values from -0.15625 to 0.15625
- key_weight: bfloat16 [1536, 128], replicated, may hold values from -0.15625 to 0.15625
- value_weight: bfloat16 [1536, 192], replicated, may hold values from -0.15625 to 0.15625
- cotangent: bfloat16 [48, 2, 768, 768], P('batch', None, 'seq'), may hold values from -6 to 6
Outputs:
- encoded: bfloat16 [48, 2, 768, 1536], P('batch', None, 'seq')
- grad_output: float32 [768, 768], P(('batch', 'segment', 'seq'))
All inputs are finite; a program needn't handle non-finite values.
Results may differ from a plain program's by a relative error of at most 0.005.
Values may be sent and summed in bfloat16 or wider, within the bound.
A program may use at most 32 MiB of HBM per device.

v0:
```python
import math

import jax
import jax.numpy as jnp
from jax import lax
from jax.sharding import PartitionSpec as P

HEADS = 4
KEY_DIM = 128
VALUE_DIM = 192


EPSILON = 1e-06


def with_halo(cells, sides, width):
    for axis, dim in sides:
        count = lax.axis_size(axis)
        ends = count - 1
        head = lax.slice_in_dim(cells, 0, width, axis=dim)
        tail = lax.slice_in_dim(cells, cells.shape[dim] - width, cells.shape[dim], axis=dim)
        cells = jnp.concatenate(
            [
                lax.ppermute(tail, axis, [(i, (i + 1) % count) for i in range(ends)]),
                cells,
                lax.ppermute(head, axis, [((i + 1) % count, i) for i in range(ends)]),
            ],
            axis=dim,
        )
    return cells


def from_behind(x, axis, by):
    length = lax.axis_size(axis)
    pairs = [(i, i + by) for i in range(length) if 0 <= i + by < length]
    return lax.ppermute(x, axis, pairs)


def rms_scale(values):
    return values * lax.rsqrt(jnp.mean(values * values, axis=-1, keepdims=True) + EPSILON)


def encode_rows(padded, depth_weight, point_weight, length_in):
    leading = padded.shape[0]
    micro = padded.shape[1]
    channels = padded.shape[3]
    summed = jnp.zeros((leading, micro, length_in // 2, channels), jnp.float32)
    for tap in range(3):
        summed = summed + depth_weight[tap].astype(jnp.float32) * padded[
            :, :, 2 * tap : 2 * tap + length_in : 2, :
        ].astype(jnp.float32)
    pooled = summed.astype(jnp.bfloat16).reshape(leading * micro * (length_in // 2), channels)
    output_rows = jax.nn.gelu(
        jnp.dot(pooled, point_weight, preferred_element_type=jnp.float32)
    ).astype(jnp.bfloat16)
    return output_rows.reshape(leading, micro, length_in // 2, point_weight.shape[1])


def project_rows(encoded, query_weight, key_weight, value_weight):
    micro = encoded.shape[1]
    positions = encoded.shape[2]
    flat_rows = encoded.reshape(micro * positions, encoded.shape[3])
    normed = rms_scale(flat_rows.astype(jnp.float32)).astype(jnp.bfloat16)
    queries = jnp.dot(normed, query_weight, preferred_element_type=jnp.float32).reshape(
        micro, positions, HEADS, KEY_DIM
    )
    queries = rms_scale(queries).astype(jnp.bfloat16)
    key_rows = rms_scale(jnp.dot(normed, key_weight, preferred_element_type=jnp.float32)).astype(
        jnp.bfloat16
    )
    value_rows = jnp.dot(normed, value_weight, preferred_element_type=jnp.float32).astype(
        jnp.bfloat16
    )
    return (
        queries,
        key_rows.reshape(micro, positions, KEY_DIM),
        value_rows.reshape(micro, positions, VALUE_DIM),
    )


def per_device(
    dna_features, depth_weight, point_weight, query_weight, key_weight, value_weight, cotangent
):
    pair_index = lax.axis_index("segment")
    first_half = pair_index == 0
    length_in = dna_features.shape[2]
    working = pair_index == 1
    out_shape = (
        dna_features.shape[0],
        dna_features.shape[1],
        length_in // 2,
        point_weight.shape[1],
    )
    padded = with_halo(dna_features, (("seq", 2),), 2)

    def run_encoder(block):
        return encode_rows(block, depth_weight, point_weight, length_in)

    def skip_encoder(block):
        return jnp.zeros(out_shape, jnp.bfloat16)

    local_rows = lax.cond(first_half, run_encoder, skip_encoder, padded)
    arrived = from_behind(local_rows, "segment", 1)
    encoded = jnp.where(first_half, local_rows, arrived)
    micro = encoded.shape[1]
    positions = encoded.shape[2]

    def run_project(block):
        return project_rows(block, query_weight, key_weight, value_weight)

    def skip_project(block):
        return (
            jnp.zeros((micro, positions, HEADS, KEY_DIM), jnp.bfloat16),
            jnp.zeros((micro, positions, KEY_DIM), jnp.bfloat16),
            jnp.zeros((micro, positions, VALUE_DIM), jnp.bfloat16),
        )

    queries, key_rows, value_rows = lax.cond(working, run_project, skip_project, encoded)
    score_scale = 1.0 / math.sqrt(KEY_DIM)
    start_state = (
        jnp.zeros((micro, positions, HEADS, VALUE_DIM), jnp.float32),
        jnp.zeros((micro, HEADS, positions), jnp.float32),
    )
    block_rows = (
        lax.all_gather(key_rows, "seq", axis=1, tiled=True),
        lax.all_gather(value_rows, "seq", axis=1, tiled=True),
    )

    def attend(state):
        scores = (
            jnp.einsum("mrhd,mpd->mhrp", queries, block_rows[0], preferred_element_type=jnp.float32)
            * score_scale
        )
        weights = jnp.exp(scores)
        denominator = jnp.sum(weights, axis=-1)
        numerator = jnp.einsum(
            "mhrp,mpe->mrhe",
            weights.astype(jnp.bfloat16),
            block_rows[1],
            preferred_element_type=jnp.float32,
        )
        return (numerator, denominator)

    def keep_state(state):
        return state

    numerator, denominator = lax.cond(working, attend, keep_state, start_state)
    safe_total = jnp.where(working, denominator, 1.0)
    attended = numerator / jnp.transpose(safe_total, (0, 2, 1))[..., None]
    attended = attended.astype(jnp.bfloat16).reshape(micro * positions, HEADS * VALUE_DIM)
    cotangent_rows = cotangent.reshape(micro * positions, cotangent.shape[3])
    batches = lax.axis_size("batch")
    norm_factor = 1.0 / math.sqrt(batches * dna_features.shape[1])
    summed = lax.psum_scatter(
        lax.dot_general(
            cotangent_rows, attended, (((0,), (0,)), ((), ())), preferred_element_type=jnp.float32
        ),
        ("batch", "segment", "seq"),
        scatter_dimension=0,
        tiled=True,
    )
    return (encoded, summed * norm_factor)


def solution(mesh):
    in_specs = (
        P("batch", None, "seq", None),
        P(),
        P(),
        P(),
        P(),
        P(),
        P("batch", None, "seq", None),
    )
    out_specs = (P("batch", None, "seq", None), P(("batch", "segment", "seq"), None))
    return jax.shard_map(
        per_device, mesh=mesh, in_specs=in_specs, out_specs=out_specs, check_vma=False
    )
```

profile of v0, /device:TPU:1, one launch (start us, length us, event | category | flops | bytes accessed | tf_op | source)
XLA Modules:
  0.0 577.1 jit_solution(15578111619803939995)
XLA Ops:
  7.2 0.0 copy-start
  7.2 0.0 copy-start.2
  7.2 0.0 copy-start.5
  7.2 0.0 all-reduce.3.cloned.1.call-start
  7.2 0.8 fusion.19
  8.1 5.6 collective-permute-start
  13.7 8.1 %collective-permute-start.1 = (bf16[1,2,2,768]{3,2,1,0:T(2,128)(2,1)S(1)}, bf16[1,2,2,768]{3,2,1,0:T(2,128)(2,1)S(1)}, u32[]{:S(2)}, u32[]{:S(2)}) collective-permute-start(bf16[1,2,2,768]{3,2,1,0:T(2,128)(2,1)S(1)} %get-tuple-element.89), channel_id=1, source_target_pairs={{1,0},{2,1},{3,2},{4,3},{5,4},{6,5},{7,6},{9,8},{10,9},{11,10},{12... | collective-permute-start | bytes 18440 | tf_op jit(solution)/shard_map/ppermute | solution.py:26
  21.8 0.0 collective-permute-done
  21.8 0.8 collective-permute-done.1
  22.6 1.2 pad_maximum_fusion
  23.8 0.0 copy-done.2
  23.9 0.0 copy-done.5
  23.9 0.0 copy-start.3
  23.9 0.0 copy-start.4
  23.9 4.9 conditional.3
  23.9 0.7 slice.17
  24.7 0.8 slice.21
  25.5 0.7 slice.19
  26.2 0.2 add_convert_fusion
  26.4 2.4 fusion.18
  28.8 0.0 copy-start.1
  28.8 2.2 collective-permute-start.2
  31.0 11.9 %collective-permute-done.2 = bf16[1,2,96,1536]{3,2,1,0:T(8,128)(2,1)} collective-permute-done((bf16[1,2,96,1536]{3,2,1,0:T(8,128)(2,1)S(1)}, bf16[1,2,96,1536]{3,2,1,0:T(8,128)(2,1)}, u32[]{:S(2)}, u32[]{:S(2)}) %collective-permute-start.2) | collective-permute-done | bytes 589856 | tf_op jit(solution)/shard_map/ppermute | solution.py:36
  42.9 0.9 broadcast_select_fusion
  43.8 0.0 copy-done.3
  43.8 0.0 copy-done.4
  43.8 0.0 copy-done.1
  43.8 0.7 conditional.4
  43.8 0.6 broadcast.87
  44.5 0.1 copy.25
  44.6 16.0 %all_gather.7 = bf16[2,768,192]{2,0,1:T(2,128)(2,1)S(1)} all-gather(bf16[2,96,192]{2,0,1:T(2,128)(2,1)S(1)} %copy.25), channel_id=1, replica_groups=mesh['batch'=48,'segment'=2,'seq'=8] {'seq'}, dimensions={1}, use_global_device_ids=true | all-gather | bytes 663552 | tf_op jit(solution)/shard_map/all_gather | solution.py:126
  60.6 15.1 %all_gather.6 = bf16[2,768,128]{2,1,0:T(8,128)(2,1)S(1)} all-gather(bf16[2,96,128]{2,1,0:T(8,128)(2,1)} %get-tuple-element.43), channel_id=1, replica_groups=mesh['batch'=48,'segment'=2,'seq'=8] {'seq'}, dimensions={1}, use_global_device_ids=true | all-gather | bytes 442368 | tf_op jit(solution)/shard_map/all_gather | solution.py:125
  75.7 0.1 conditional.5
  75.7 0.1 broadcast_in_dim.7
  75.8 0.2 divide_convert_fusion
  76.0 0.3 copy.27
  76.3 0.3 reshape.105
  76.7 0.0 copy-done
  76.7 1.9 convolution_bitcast_fusion.1
  78.6 0.0 all-reduce.3.cloned.1.call-update
  78.6 489.7 %all-reduce.3.cloned.1.call-done = f32[768,768]{0,1:T(8,128)} async-done(((f32[768,768]{0,1:T(8,128)}), f32[768,768]{0,1:T(8,128)}) %all-reduce.3.cloned.1.call-update) | async-done | bytes 2359312
  568.3 1.2 dynamic-slice_multiply_fusion
  569.5 0.7 copy.28
  (5 shorter events, 0.1 us)
Async XLA Ops:
  7.2 69.5 %copy-start = (bf16[1,2,96,768]{3,2,1,0:T(8,128)(2,1)S(1)}, bf16[1,2,96,768]{3,2,1,0:T(8,128)(2,1)}, u32[]{:S(2)}) copy-start(bf16[1,2,96,768]{3,2,1,0:T(8,128)(2,1)} %param.19) | copy-start | bytes 884740
  7.2 16.7 %copy-start.2 = (bf16[1,2,192,768]{3,2,1,0:T(8,128)(2,1)S(1)}, bf16[1,2,192,768]{3,2,1,0:T(8,128)(2,1)}, u32[]{:S(2)}) copy-start(bf16[1,2,192,768]{3,2,1,0:T(8,128)(2,1)} %param.13) | copy-start | bytes 1769476
  7.2 16.7 %copy-start.5 = (bf16[3,768]{1,0:T(4,128)(2,1)S(1)}, bf16[3,768]{1,0:T(4,128)(2,1)}, u32[]{:S(2)}) copy-start(bf16[3,768]{1,0:T(4,128)(2,1)} %param.14) | copy-start | bytes 13828
  7.2 561.1 %all-reduce.3.cloned.1.call-start = ((), (), s32[]{:S(2)}) async-start(), calls=%async_computation | async-start | bytes 4718592
  8.1 13.7 %collective-permute-start = (bf16[1,2,2,768]{3,2,1,0:T(2,128)(2,1)S(1)}, bf16[1,2,2,768]{3,2,1,0:T(2,128)(2,1)S(1)}, u32[]{:S(2)}, u32[]{:S(2)}) collective-permute-start(bf16[1,2,2,768]{3,2,1,0:T(2,128)(2,1)S(1)} %get-tuple-element.88), channel_id=1, source_target_pairs={{0,1},{1,2},{2,3},{3,4},{4,5},{5,6},{6,7},{8,9},{9,10},{10,11},{11... | collective-permute-start | bytes 18440 | tf_op jit(solution)/shard_map/ppermute | solution.py:24
  13.7 8.9 %collective-permute-start.1 = (bf16[1,2,2,768]{3,2,1,0:T(2,128)(2,1)S(1)}, bf16[1,2,2,768]{3,2,1,0:T(2,128)(2,1)S(1)}, u32[]{:S(2)}, u32[]{:S(2)}) collective-permute-start(bf16[1,2,2,768]{3,2,1,0:T(2,128)(2,1)S(1)} %get-tuple-element.89), channel_id=1, source_target_pairs={{1,0},{2,1},{3,2},{4,3},{5,4},{6,5},{7,6},{9,8},{10,9},{11,10},{12... | collective-permute-start | bytes 18440 | tf_op jit(solution)/shard_map/ppermute | solution.py:26
  23.9 19.9 %copy-start.3 = (bf16[1536,192]{0,1:T(8,128)(2,1)S(1)}, bf16[1536,192]{0,1:T(8,128)(2,1)}, u32[]{:S(2)}) copy-start(bf16[1536,192]{0,1:T(8,128)(2,1)} %param.18) | copy-start | bytes 1769476
  23.9 19.9 %copy-start.4 = (bf16[1536,128]{1,0:T(8,128)(2,1)S(1)}, bf16[1536,128]{1,0:T(8,128)(2,1)}, u32[]{:S(2)}) copy-start(bf16[1536,128]{1,0:T(8,128)(2,1)} %param.17) | copy-start | bytes 1179652
  28.8 15.0 %copy-start.1 = (bf16[1536,512]{1,0:T(8,128)(2,1)S(1)}, bf16[1536,512]{1,0:T(8,128)(2,1)}, u32[]{:S(2)}) copy-start(bf16[1536,512]{1,0:T(8,128)(2,1)} %param.16) | copy-start | bytes 4718596
  28.8 14.1 %collective-permute-start.2 = (bf16[1,2,96,1536]{3,2,1,0:T(8,128)(2,1)S(1)}, bf16[1,2,96,1536]{3,2,1,0:T(8,128)(2,1)}, u32[]{:S(2)}, u32[]{:S(2)}) collective-permute-start(bf16[1,2,96,1536]{3,2,1,0:T(8,128)(2,1)S(1)} %get-tuple-element.100), channel_id=1, source_target_pairs={{0,8},{1,9},{2,10},{3,11},{4,12},{5,13},{6,14},{7,15},{16,24},{17,... | collective-permute-start | bytes 1769480 | tf_op jit(solution)/shard_map/ppermute | solution.py:36
Sparse Core Ops, SparseCore 0:
  78.7 489.5 all-reduce.2
where the time goes:
time: 578 us; the launch traced here: 577 us
  waiting for transfers between devices  502 us (87%)
  blocking collectives  31.1 us (5%)
  starting transfers between devices  16 us (3%)
  between operations  14.2 us (2%)
    unnamed x2, waiting for transfers between devices  490 us
    all_gather x1, blocking collectives, per_device(): lax.all_gather(value_rows, 'seq', axis=1, tiled=True)  16 us
    all_gather x1, blocking collectives, per_device(): lax.all_gather(key_rows, 'seq', axis=1, tiled=True)  15.1 us
    ppermute x1, waiting for transfers between devices, from_behind(): return lax.ppermute(x, axis, pairs)  11.9 us
  transfers between devices with their start and end apart: 4, of which 3 were waited for; matrix products, arithmetic and copies ran while one was open for 0% of the time, Pallas kernels for 0%

commit v1 on v0

v1 whole, which is shorter than its diff:
```python
import functools
import math

import jax
import jax.numpy as jnp
from jax import lax
from jax.experimental import pallas as pl
from jax.experimental.pallas import tpu as pltpu
from jax.sharding import PartitionSpec as P

MESH = pl.DeviceIdType.MESH
F32 = jnp.float32
BF16 = jnp.bfloat16

C_IN = 768
D = 1536
KEY = 128
VAL = 192
ROWS = 96
X, Z, S = 4, 12, 8
EPSILON = 1e-06
LANE = 128
COL = 256
KV_W = 384
EXP2_SCALE = math.log2(math.e) / math.sqrt(KEY)


def gelu(u):
    inner = math.sqrt(2.0 / math.pi) * (u + 0.044715 * (u * u * u))
    return 0.5 * u * (1.0 + jnp.tanh(inner))


def rms_of(values):
    return lax.rsqrt(jnp.mean(values * values, axis=-1, keepdims=True) + EPSILON)


def kernel(
    norm,
    dna, dw, pw, qw, kw, vw, cot,
    enc_out, grad_out,
    xin, dwv, pwv, qwv, kwv, vwv, cotv,
    xf, ext, pooled, enc, ssq, rinv, qacc, kacc, vacc,
    hs, hr, q4, qall, kvs, kvbuf, acc, cott, att2, psend, p1r, red1, p2s, p2r, p3s, p3r,
    in_sem, enc_sem, h_send, h_recv, cot_send, cot_recv, q_send, q_recv,
    d_send, d_recv, r_send, r_recv, p1_send, p1_recv, p2_send, p2_recv, p3_send, p3_recv,
):
    b, g, s = lax.axis_index("batch"), lax.axis_index("segment"), lax.axis_index("seq")
    x, z = b // Z, lax.rem(b, Z)
    h, c = s // 2, lax.rem(s, 2)
    other = 1 - g
    sign = 2 * g - 1
    sib = (b, g, h * 2 + (1 - c))

    def gx_peer(dx, dg):
        return (lax.rem(x + dx, X) * Z + z, lax.rem(g + dg, 2), s)

    def s_peer(d):
        return (b, g, lax.rem(s + d, S))

    def z_peer(d):
        return (x * Z + lax.rem(z + d, Z), g, s)

    near = (b, other, lax.rem(h + sign + 4, 4) * 2 + c)
    middle = (b, g, lax.rem(h + sign + 4, 4) * 2 + c)
    far = (b, other, lax.rem(h + 2, 4) * 2 + c)

    loads = [
        pltpu.make_async_copy(dna.at[0], xin, in_sem.at[0]),
        pltpu.make_async_copy(dw, dwv, in_sem.at[1]),
        pltpu.make_async_copy(cot.at[0, g], cotv.at[0], in_sem.at[2]),
        pltpu.make_async_copy(pw, pwv, in_sem.at[3]),
        pltpu.make_async_copy(kw, kwv, in_sem.at[4]),
        pltpu.make_async_copy(vw, vwv, in_sem.at[5]),
        pltpu.make_async_copy(qw, qwv, in_sem.at[6]),
    ]
    for load in loads:
        load.start()

    barrier = pltpu.get_barrier_semaphore()

    def hello(device):
        pl.semaphore_signal(barrier, inc=1, device_id=device, device_id_type=MESH)

    for d in range(1, Z):
        hello(z_peer(d))
    for d in range(1, 8):
        hello(gx_peer(d // 2, d % 2))
    for d in range(1, S):
        hello(s_peer(d))
    hello(near)
    hello(far)

    loads[0].wait()
    for m in range(2):
        for k in range(6):
            i = m * 6 + k
            xf[k] = xin[m, :, k * LANE : (k + 1) * LANE].astype(F32)
            even = xf[k, pl.ds(0, ROWS, stride=2), :]
            ext[i, 8 : 8 + ROWS, :] = even
            hs[0, i] = even[0:1]
            hs[1, i] = even[ROWS - 1 : ROWS]
    lane = lax.broadcasted_iota(jnp.int32, (ROWS, LANE), 1)
    ones = jnp.where(lane >= VAL - LANE, 1.0, 0.0).astype(BF16)
    for m in range(2):
        kvs[m, :, 2 * LANE : 3 * LANE] = ones
    loads[1].wait()
    loads[2].wait()

    pl.semaphore_wait(barrier, 11 + 7 + 7 + 2)

    to_left = pltpu.make_async_remote_copy(
        src_ref=hs.at[0], dst_ref=hr.at[1], send_sem=h_send.at[0], recv_sem=h_recv.at[1],
        device_id=s_peer(S - 1), device_id_type=MESH,
    )
    to_right = pltpu.make_async_remote_copy(
        src_ref=hs.at[1], dst_ref=hr.at[0], send_sem=h_send.at[1], recv_sem=h_recv.at[0],
        device_id=s_peer(1), device_id_type=MESH,
    )
    to_left.start()
    to_right.start()
    cot_copy = pltpu.make_async_remote_copy(
        src_ref=cotv.at[0], dst_ref=cotv.at[1], send_sem=cot_send, recv_sem=cot_recv,
        device_id=sib, device_id_type=MESH,
    )
    cot_copy.start()
    to_left.wait()
    to_right.wait()

    w = dwv[...].astype(F32)
    for m in range(2):
        for k in range(6):
            i = m * 6 + k
            ext[i, 7:8, :] = jnp.where(s > 0, hr[0, i], 0.0)
            ext[i, 8 + ROWS : 9 + ROWS, :] = jnp.where(s < S - 1, hr[1, i], 0.0)
            part = slice(k * LANE, (k + 1) * LANE)
            total = w[0:1, part] * ext[i, 7 : 7 + ROWS, :]
            total = total + w[1:2, part] * ext[i, 8 : 8 + ROWS, :]
            total = total + w[2:3, part] * ext[i, 9 : 9 + ROWS, :]
            pooled[m * ROWS : (m + 1) * ROWS, part] = total.astype(BF16)

    for load in loads[3:]:
        load.wait()
    ssq[...] = jnp.zeros_like(ssq)
    qacc[...] = jnp.zeros_like(qacc)
    kacc[...] = jnp.zeros_like(kacc)
    vacc[...] = jnp.zeros_like(vacc)

    def encode(n, _):
        cols = pl.ds(pl.multiple_of(n * COL, COL), COL)
        u = jnp.dot(pooled[...], pwv[:, cols], preferred_element_type=F32)
        rows = gelu(u).astype(BF16)
        enc[n] = rows.reshape(2, ROWS, COL)
        wide = rows.astype(F32)
        square = wide * wide
        ssq[...] += square[:, :LANE] + square[:, LANE:]
        kacc[...] += jnp.dot(rows, kwv[cols, :], preferred_element_type=F32)
        vacc[...] += jnp.dot(rows, vwv[cols, :], preferred_element_type=F32)
        qacc[...] += jnp.dot(enc[n, g], qwv[cols, :], preferred_element_type=F32)
        pltpu.make_async_copy(enc.at[n], enc_out.at[0, :, :, cols], enc_sem.at[n]).start()
        return 0

    lax.fori_loop(0, D // COL, encode, 0)

    scale = lax.rsqrt(jnp.sum(ssq[...], axis=-1, keepdims=True) * (1.0 / D) + EPSILON)
    rinv[...] = jnp.broadcast_to(scale, (2 * ROWS, LANE)).reshape(2, ROWS, LANE)
    keys = kacc[...] * scale
    keys = (keys * rms_of(keys)).astype(BF16)
    values = (vacc[...] * scale).astype(BF16)
    for m in range(2):
        kvs[m, :, :KEY] = keys[m * ROWS : (m + 1) * ROWS]
        kvs[m, :, KEY : KEY + VAL] = values[m * ROWS : (m + 1) * ROWS]

    def kv_copy(j, block, slot, device):
        return pltpu.make_async_remote_copy(
            src_ref=kvs.at[block], dst_ref=kvbuf.at[slot], send_sem=d_send.at[j],
            recv_sem=d_recv.at[j], device_id=device, device_id_type=MESH,
        )

    def relay(j, source):
        return pltpu.make_async_remote_copy(
            src_ref=source, dst_ref=kvbuf.at[2 * j + 1], send_sem=r_send.at[j],
            recv_sem=r_recv.at[j], device_id=sib, device_id_type=MESH,
        )

    direct = [kv_copy(0, other, 2, near), kv_copy(1, g, 4, middle), kv_copy(2, other, 6, far)]
    for copy in direct:
        copy.start()
    relays = [relay(0, kvs.at[g])]
    relays[0].start()
    kvbuf[0] = kvs[g]

    row_scale = rinv[g]
    for i in range(4):
        query = qacc[:, i * KEY : (i + 1) * KEY] * row_scale
        q4[i] = (query * rms_of(query)).astype(BF16)
    q_copy = pltpu.make_async_remote_copy(
        src_ref=q4.at[pl.ds(2 * (1 - c), 2)], dst_ref=qall.at[:, 1], send_sem=q_send,
        recv_sem=q_recv, device_id=sib, device_id_type=MESH,
    )
    q_copy.start()
    qall[:, 0] = q4[pl.ds(2 * c, 2)]

    cot_copy.wait()
    turned = jnp.transpose(cotv[...].reshape(2 * ROWS, C_IN))
    cott[...] = turned.reshape(X, 2 * ROWS, 2 * ROWS)

    def attend(j):
        block = kvbuf[2 * j : 2 * j + 2].reshape(2 * ROWS, KV_W)
        query = qall[...].reshape(4 * ROWS, KEY)
        scores = lax.dot_general(
            query, block[:, :KEY], (((1,), (1,)), ((), ())), preferred_element_type=F32
        )
        weights = jnp.exp2(scores * EXP2_SCALE).astype(BF16)
        part = jnp.dot(weights, block[:, KEY:], preferred_element_type=F32)
        if j == 0:
            acc[...] = part
        else:
            acc[...] += part

    def pass_on(j):
        direct[j - 1].wait_recv()
        relays.append(relay(j, kvbuf.at[2 * j]))
        relays[j].start()

    q_copy.wait_recv()
    relays[0].wait_recv()
    attend(0)
    pass_on(1)
    pass_on(2)
    relays[1].wait_recv()
    attend(1)
    pass_on(3)
    relays[2].wait_recv()
    attend(2)
    relays[3].wait_recv()
    attend(3)

    total = acc[...]
    attended = (total[:, :VAL] / total[:, VAL : VAL + 1]).astype(BF16)
    att2[...] = jnp.concatenate([attended[: 2 * ROWS], attended[2 * ROWS :]], axis=1)

    def p1_copy(dx, dg):
        i = dx * 2 + dg
        return pltpu.make_async_remote_copy(
            src_ref=psend.at[i], dst_ref=p1r.at[i], send_sem=p1_send.at[i],
            recv_sem=p1_recv.at[i], device_id=gx_peer(dx, dg), device_id_type=MESH,
        )

    for dx in (2, 1, 3, 0):
        share = jnp.dot(cott[lax.rem(x + dx, X)], att2[...], preferred_element_type=F32)
        share = share.reshape(Z, 2, S, 2 * VAL)
        low, high = share[:, 0].reshape(Z * S, 2 * VAL), share[:, 1].reshape(Z * S, 2 * VAL)
        same, cross = jnp.where(g == 0, low, high), jnp.where(g == 0, high, low)
        psend[dx * 2 + 1] = cross.astype(BF16)
        p1_copy(dx, 1).start()
        psend[dx * 2] = same.astype(BF16)
        if dx > 0:
            p1_copy(dx, 0).start()
    total = psend[0].astype(F32)
    for i in (1, 2, 3, 6, 7, 4, 5):
        p1_copy(i // 2, i % 2).wait_recv()
        total = total + p1r[i].astype(F32)

    for k in range(3):
        red1[k, : Z * S, :] = total[:, k * LANE : (k + 1) * LANE]
        red1[k, Z * S :, :] = jnp.zeros((S * 16 - Z * S, LANE), F32)
    for i in range(S):
        for k in range(3):
            p2s[i, :, k * LANE : (k + 1) * LANE] = red1[k, pl.ds(i, 16, stride=S), :].astype(BF16)

    def p2_copy(d):
        return pltpu.make_async_remote_copy(
            src_ref=p2s.at[lax.rem(s + d, S)], dst_ref=p2r.at[d], send_sem=p2_send.at[d],
            recv_sem=p2_recv.at[d], device_id=s_peer(d), device_id_type=MESH,
        )

    for d in (4, 3, 5, 2, 6, 1, 7):
        p2_copy(d).start()
    mine, theirs = p2s[s].astype(F32), None
    for d in (1, 7, 2, 6, 3, 5, 4):
        p2_copy(d).wait_recv()
        block = p2r[d].astype(F32)
        if d % 2 == 0:
            mine = mine + block
        else:
            theirs = block if theirs is None else theirs + block

    for i in range(Z):
        p3s[c, i] = mine[i : i + 1]
        p3s[1 - c, i] = theirs[i : i + 1]

    def p3_copy(d):
        return pltpu.make_async_remote_copy(
            src_ref=p3s.at[:, lax.rem(z + d, Z)], dst_ref=p3r.at[d], send_sem=p3_send.at[d],
            recv_sem=p3_recv.at[d], device_id=z_peer(d), device_id_type=MESH,
        )

    for d in (6, 5, 7, 4, 8, 3, 9, 2, 10, 1, 11):
        p3_copy(d).start()
    row = p3s[:, z]
    for d in (1, 11, 2, 10, 3, 9, 4, 8, 5, 7, 6):
        p3_copy(d).wait_recv()
        row = row + p3r[d]
    row = row * norm
    grad_out[:, : 2 * VAL] = row[0]
    grad_out[:, 2 * VAL :] = row[1]

    cols = pl.ds(0, COL)
    for n in range(D // COL):
        pltpu.make_async_copy(enc.at[n], enc_out.at[0, :, :, cols], enc_sem.at[n]).wait()
    for copy in direct + relays + [q_copy]:
        copy.wait_send()
    for i in range(1, 8):
        p1_copy(i // 2, i % 2).wait_send()
        p2_copy(i).wait_send()
    for d in range(1, Z):
        p3_copy(d).wait_send()


def per_device(dna, dw, pw, qw, kw, vw, cot):
    norm = 1.0 / math.sqrt(X * Z * dna.shape[1])
    dma = pltpu.SemaphoreType.DMA
    vmem = pltpu.VMEM
    anywhere = pl.BlockSpec(memory_space=pl.ANY)
    return pl.pallas_call(
        functools.partial(kernel, norm),
        out_shape=(
            jax.ShapeDtypeStruct((1, 2, ROWS, D), BF16),
            jax.ShapeDtypeStruct((1, 4 * VAL), F32),
        ),
        in_specs=[anywhere] * 7,
        out_specs=(anywhere, pl.BlockSpec(memory_space=pltpu.VMEM)),
        scratch_shapes=[
            vmem((2, 2 * ROWS, C_IN), BF16),
            vmem((3, C_IN), BF16),
            vmem((C_IN, D), BF16),
            vmem((D, 4 * KEY), BF16),
            vmem((D, KEY), BF16),
            vmem((D, VAL), BF16),
            vmem((2, ROWS, C_IN), BF16),
            vmem((6, 2 * ROWS, LANE), F32),
            vmem((12, ROWS + 16, LANE), F32),
            vmem((2 * ROWS, C_IN), BF16),
            vmem((D // COL, 2, ROWS, COL), BF16),
            vmem((2 * ROWS, LANE), F32),
            vmem((2, ROWS, LANE), F32),
            vmem((ROWS, 4 * KEY), F32),
            vmem((2 * ROWS, KEY), F32),
            vmem((2 * ROWS, VAL), F32),
            vmem((2, 12, 1, LANE), F32),
            vmem((2, 12, 1, LANE), F32),
            vmem((4, ROWS, KEY), BF16),
            vmem((2, 2, ROWS, KEY), BF16),
            vmem((2, ROWS, KV_W), BF16),
            vmem((8, ROWS, KV_W), BF16),
            vmem((4 * ROWS, COL), F32),
            vmem((X, 2 * ROWS, 2 * ROWS), BF16),
            vmem((2 * ROWS, 2 * VAL), BF16),
            vmem((8, Z * S, 2 * VAL), BF16),
            vmem((8, Z * S, 2 * VAL), BF16),
            vmem((3, 16 * S, LANE), F32),
            vmem((S, 16, 2 * VAL), BF16),
            vmem((S, 16, 2 * VAL), BF16),
            vmem((2, Z, 1, 2 * VAL), F32),
            vmem((Z, 2, 1, 2 * VAL), F32),
            dma((7,)), dma((D // COL,)), dma((2,)), dma((2,)), dma, dma, dma, dma,
            dma((3,)), dma((3,)), dma((4,)), dma((4,)), dma((8,)), dma((8,)), dma((8,)), dma((8,)),
            dma((Z,)), dma((Z,)),
        ],
        compiler_params=pltpu.CompilerParams(
            collective_id=0, has_side_effects=True, vmem_limit_bytes=40 * 2**20
        ),
        name="window_step",
    )(dna, dw, pw, qw, kw, vw, cot)


def solution(mesh):
    rows = P("batch", None, "seq", None)
    return jax.shard_map(
        per_device,
        mesh=mesh,
        in_specs=(rows, P(), P(), P(), P(), P(), rows),
        out_specs=(rows, P(("batch", "segment", "seq"), None)),
        check_vma=False,
    )
```

time: 578 us -> 68.9 us (0.12)
  waiting for transfers between devices: 502 us -> 0 us
  Pallas kernels: 0 us -> 58.4 us
  blocking collectives: 31.1 us -> 0 us
  starting transfers between devices: 16 us -> 0 us
  between operations: 14.2 us -> 0.66 us
    unnamed x2 -> x0, waiting for transfers between devices: 490 us -> none
    pallas_call x0 -> x1, Pallas kernels: none -> 58.4 us  [per_device(): pl.pallas_call(functools.partial(kernel, norm), out_shape=(jax.ShapeDtype...]
    all_gather x2 -> x0, blocking collectives: 31.1 us -> none  [the longest x1 16 us: per_device(): lax.all_gather(value_rows, 'seq', axis=1, tiled=True)]
    ppermute x3 -> x0, starting transfers between devices: 16 us -> none  [the longest x1 8.11 us: with_halo(): lax.ppermute(head, axis, [((i + 1) % count, i) for i in range(ends)])]
    ppermute x3 -> x0, waiting for transfers between devices: 12.7 us -> none  [the longest x1 11.9 us: from_behind(): return lax.ppermute(x, axis, pairs)]
    unnamed x13 -> x15, local copies, waits for them, and re-layouts: 0.77 us -> 9.51 us
  transfers between devices with their start and end apart: 4 -> 0, of which waited for: 3 -> 0; matrix products, arithmetic and copies ran while one was open for 0% -> 0% of each run, Pallas kernels for 0% -> 0%
where the time goes in v1:
time: 68.9 us; the launch traced here: 68.5 us
  Pallas kernels  58.4 us (85%)
  local copies, waits for them, and re-layouts  9.51 us (14%)
    pallas_call x1, Pallas kernels, per_device(): pl.pallas_call(functools.partial(kernel, norm), out_shape=(jax.ShapeDtype...  58.4 us
    unnamed x15, local copies, waits for them, and re-layouts  9.51 us

profile of v1, /device:TPU:1, one launch (start us, length us, event | category | flops | bytes accessed | tf_op | source)
XLA Modules:
  0.0 68.5 jit_solution(6126128350710931908)
XLA Ops:
  0.6 1.3 %copy.9.vw = bf16[1536,192]{1,0:T(8,128)(2,1)S(1)} copy(bf16[1536,192]{0,1:T(8,128)(2,1)} %param.12) | data formatting | bytes 1179648 | tf_op args[5]
  2.0 0.0 copy-start
  2.0 1.7 %copy-done = bf16[768,1536]{1,0:T(8,128)(2,1)S(1)} copy-done((bf16[768,1536]{1,0:T(8,128)(2,1)S(1)}, bf16[768,1536]{1,0:T(8,128)(2,1)}, u32[]{:S(2)}) %copy-start) | copy-done | bytes 2359320
  3.6 0.0 copy-start.1
  3.6 1.4 %copy-done.1 = bf16[1536,512]{1,0:T(8,128)(2,1)S(1)} copy-done((bf16[1536,512]{1,0:T(8,128)(2,1)S(1)}, bf16[1536,512]{1,0:T(8,128)(2,1)}, u32[]{:S(2)}) %copy-start.1) | copy-done | bytes 1572888
  5.0 0.0 copy-start.2
  5.0 1.1 %copy-done.2 = bf16[1,2,192,768]{3,2,1,0:T(8,128)(2,1)S(1)} copy-done((bf16[1,2,192,768]{3,2,1,0:T(8,128)(2,1)S(1)}, bf16[1,2,192,768]{3,2,1,0:T(8,128)(2,1)}, u32[]{:S(2)}) %copy-start.2) | copy-done | bytes 589848
  6.1 0.0 copy-start.3
  6.1 1.0 %copy-done.3 = bf16[1536,128]{1,0:T(8,128)(2,1)S(1)} copy-done((bf16[1536,128]{1,0:T(8,128)(2,1)S(1)}, bf16[1536,128]{1,0:T(8,128)(2,1)}, u32[]{:S(2)}) %copy-start.3) | copy-done | bytes 393240
  7.1 0.0 copy-start.4
  7.1 1.0 %copy-done.4 = bf16[1,2,96,768]{3,2,1,0:T(8,128)(2,1)S(1)} copy-done((bf16[1,2,96,768]{3,2,1,0:T(8,128)(2,1)S(1)}, bf16[1,2,96,768]{3,2,1,0:T(8,128)(2,1)}, u32[]{:S(2)}) %copy-start.4) | copy-done | bytes 294936
  8.1 0.0 copy-start.5
  8.1 0.7 %copy-done.5 = bf16[3,768]{1,0:T(4,128)(2,1)S(1)} copy-done((bf16[3,768]{1,0:T(4,128)(2,1)S(1)}, bf16[3,768]{1,0:T(4,128)(2,1)}, u32[]{:S(2)}) %copy-start.5) | copy-done | bytes 4632
  8.8 58.4 %window_step.1 = (bf16[1,2,96,1536]{3,2,1,0:T(8,128)(2,1)S(1)}, f32[1,768]{1,0:T(1,128)S(1)}) custom-call(bf16[1,2,192,768]{3,2,1,0:T(8,128)(2,1)S(1)} %copy-done.2, bf16[3,768]{1,0:T(4,128)(2,1)S(1)} %copy-done.5, bf16[768,1536]{1,0:T(8,128)(2,1)S(1)} %copy-done, bf16[1536,512]{1,0:T(8,128)(2,1)S(1)} %copy-done.1, bf16[1536,128]{1,0:T(8,128)(2,1)S(1)} %copy-done.3, ...), custom_call_target="tpu_custom_call" | custom-call | tf_op jit(solution)/shard_map/window_step/pallas_call | solution.py:325
  67.1 0.8 %copy.12 = bf16[1,2,96,1536]{3,2,1,0:T(8,128)(2,1)} copy(bf16[1,2,96,1536]{3,2,1,0:T(8,128)(2,1)S(1)} %get-tuple-element.4) | data formatting | bytes 1179648
  67.9 0.6 copy.13
Async XLA Ops:
  2.0 1.7 %copy-start = (bf16[768,1536]{1,0:T(8,128)(2,1)S(1)}, bf16[768,1536]{1,0:T(8,128)(2,1)}, u32[]{:S(2)}) copy-start(bf16[768,1536]{1,0:T(8,128)(2,1)} %pw.1) | copy-start | bytes 7077892
  3.6 1.4 %copy-start.1 = (bf16[1536,512]{1,0:T(8,128)(2,1)S(1)}, bf16[1536,512]{1,0:T(8,128)(2,1)}, u32[]{:S(2)}) copy-start(bf16[1536,512]{1,0:T(8,128)(2,1)} %qw.1) | copy-start | bytes 4718596
  5.0 1.1 %copy-start.2 = (bf16[1,2,192,768]{3,2,1,0:T(8,128)(2,1)S(1)}, bf16[1,2,192,768]{3,2,1,0:T(8,128)(2,1)}, u32[]{:S(2)}) copy-start(bf16[1,2,192,768]{3,2,1,0:T(8,128)(2,1)} %dna.1) | copy-start | bytes 1769476
  6.1 1.0 %copy-start.3 = (bf16[1536,128]{1,0:T(8,128)(2,1)S(1)}, bf16[1536,128]{1,0:T(8,128)(2,1)}, u32[]{:S(2)}) copy-start(bf16[1536,128]{1,0:T(8,128)(2,1)} %kw.1) | copy-start | bytes 1179652
  7.1 1.0 %copy-start.4 = (bf16[1,2,96,768]{3,2,1,0:T(8,128)(2,1)S(1)}, bf16[1,2,96,768]{3,2,1,0:T(8,128)(2,1)}, u32[]{:S(2)}) copy-start(bf16[1,2,96,768]{3,2,1,0:T(8,128)(2,1)} %cot.1) | copy-start | bytes 884740
  8.1 0.7 %copy-start.5 = (bf16[3,768]{1,0:T(4,128)(2,1)S(1)}, bf16[3,768]{1,0:T(4,128)(2,1)}, u32[]{:S(2)}) copy-start(bf16[3,768]{1,0:T(4,128)(2,1)} %dw.1) | copy-start | bytes 13828

commit v2 on v1

v2 whole, which is shorter than its diff:
```python
import functools
import math

import jax
import jax.numpy as jnp
from jax import lax
from jax.experimental import pallas as pl
from jax.experimental.pallas import tpu as pltpu
from jax.sharding import PartitionSpec as P

MESH = pl.DeviceIdType.MESH
F32 = jnp.float32
BF16 = jnp.bfloat16

C_IN = 768
D = 1536
KEY = 128
VAL = 192
ROWS = 96
X, Z, S = 4, 12, 8
EPSILON = 1e-06
LANE = 128
COL = 256
KV_ROWS = 2 * ROWS + ROWS // 2
EXP2_SCALE = math.log2(math.e) / math.sqrt(KEY)


def gelu(u):
    inner = math.sqrt(2.0 / math.pi) * (u + 0.044715 * (u * u * u))
    return 0.5 * u * (1.0 + jnp.tanh(inner))


def rms_of(values):
    return lax.rsqrt(jnp.mean(values * values, axis=-1, keepdims=True) + EPSILON)


def kernel(
    norm,
    dna, dw, pw, qw, kw, vw, cot,
    enc_out, grad_out,
    xin, dwv, pwv, qwv, kwv, vwv, cotv,
    xf, ext, pooled, enc, ssq, rinv, qacc, kacc, vacc,
    hs, hr, q4, qall, kvs, kvbuf, acc, cott, attx, psend, p1r, red1, p2s, p2r, p3s, p3r,
    in_sem, enc_sem, h_send, h_recv, cot_send, cot_recv, q_send, q_recv,
    d_send, d_recv, r_send, r_recv, a_send, a_recv,
    p1_send, p1_recv, p2_send, p2_recv, p3_send, p3_recv, met1, met2, met3,
):
    b, g, s = lax.axis_index("batch"), lax.axis_index("segment"), lax.axis_index("seq")
    x, z = b // Z, lax.rem(b, Z)
    h, c = s // 2, lax.rem(s, 2)
    other = 1 - g
    sign = 2 * g - 1

    def x_peer(d):
        return (lax.rem(x + d, X) * Z + z, g, s)

    def s_peer(d):
        return (b, g, lax.rem(s + d, S))

    def z_peer(d):
        return (x * Z + lax.rem(z + d, Z), g, s)

    sib = (b, g, h * 2 + (1 - c))
    partner = (b, other, s)
    near = (b, other, lax.rem(h + sign + 4, 4) * 2 + c)
    ahead = (b, g, lax.rem(h + sign + 4, 4) * 2 + c)
    behind = (b, g, lax.rem(h - sign + 4, 4) * 2 + c)
    cross = (b, g, lax.rem(s + 2 * c - 1 + S, S))

    def signal(semaphore, devices):
        for device in devices:
            pl.semaphore_signal(semaphore, inc=1, device_id=device, device_id_type=MESH)

    barrier = pltpu.get_barrier_semaphore()
    beside = [partner, near, x_peer(1), x_peer(X - 1), z_peer(1), z_peer(Z - 1)]
    signal(barrier, [cross, sib] + beside)

    loads = [
        pltpu.make_async_copy(dna.at[0], xin, in_sem.at[0]),
        pltpu.make_async_copy(dw, dwv, in_sem.at[1]),
        pltpu.make_async_copy(pw, pwv, in_sem.at[2]),
        pltpu.make_async_copy(kw, kwv, in_sem.at[3]),
        pltpu.make_async_copy(vw, vwv, in_sem.at[4]),
        pltpu.make_async_copy(qw, qwv, in_sem.at[5]),
        pltpu.make_async_copy(cot.at[0, g], cotv.at[0, 0], in_sem.at[6]),
        pltpu.make_async_copy(cot.at[0, other], cotv.at[1, 0], in_sem.at[7]),
    ]
    for load in loads:
        load.start()

    loads[0].wait()
    for m in range(2):
        for k in range(6):
            i = m * 6 + k
            xf[k] = xin[m, :, k * LANE : (k + 1) * LANE].astype(F32)
            even = xf[k, pl.ds(0, ROWS, stride=2), :]
            ext[i, 8 : 8 + ROWS, :] = even
            hs[0, i] = even[0:1]
            hs[1, i] = even[ROWS - 1 : ROWS]

    pl.semaphore_wait(barrier, 8)
    to_left = pltpu.make_async_remote_copy(
        src_ref=hs.at[0], dst_ref=hr.at[1], send_sem=h_send.at[0], recv_sem=h_recv.at[1],
        device_id=s_peer(S - 1), device_id_type=MESH,
    )
    to_right = pltpu.make_async_remote_copy(
        src_ref=hs.at[1], dst_ref=hr.at[0], send_sem=h_send.at[1], recv_sem=h_recv.at[0],
        device_id=s_peer(1), device_id_type=MESH,
    )
    to_left.start()
    to_right.start()
    signal(met1, beside)
    loads[1].wait()
    w = dwv[...].astype(F32)
    to_left.wait()
    to_right.wait()

    for m in range(2):
        for k in range(6):
            i = m * 6 + k
            ext[i, 7:8, :] = jnp.where(s > 0, hr[0, i], 0.0)
            ext[i, 8 + ROWS : 9 + ROWS, :] = jnp.where(s < S - 1, hr[1, i], 0.0)
            part = slice(k * LANE, (k + 1) * LANE)
            total = w[0:1, part] * ext[i, 7 : 7 + ROWS, :]
            total = total + w[1:2, part] * ext[i, 8 : 8 + ROWS, :]
            total = total + w[2:3, part] * ext[i, 9 : 9 + ROWS, :]
            pooled[m * ROWS : (m + 1) * ROWS, part] = total.astype(BF16)

    pl.semaphore_wait(met1, 6)
    signal(met2, [ahead, behind, z_peer(2), z_peer(Z - 2)])
    loads[6].wait()
    loads[7].wait()
    cot_copy = pltpu.make_async_remote_copy(
        src_ref=cotv.at[:, 0], dst_ref=cotv.at[:, 1], send_sem=cot_send, recv_sem=cot_recv,
        device_id=sib, device_id_type=MESH,
    )
    cot_copy.start()
    for load in loads[2:6]:
        load.wait()

    for n in range(D // COL):
        cols = slice(n * COL, (n + 1) * COL)
        u = jnp.dot(pooled[...], pwv[:, cols], preferred_element_type=F32)
        rows = gelu(u).astype(BF16)
        enc[n] = rows.reshape(2, ROWS, COL)
        pltpu.make_async_copy(enc.at[n], enc_out.at[0, :, :, cols], enc_sem.at[n]).start()
        wide = rows.astype(F32)
        square = wide * wide
        square = square[:, :LANE] + square[:, LANE:]
        key_part = jnp.dot(rows, kwv[cols, :], preferred_element_type=F32)
        value_part = lax.dot_general(
            rows, vwv[:, cols], (((1,), (1,)), ((), ())), preferred_element_type=F32
        )
        query_part = jnp.dot(enc[n, g], qwv[cols, :], preferred_element_type=F32)
        if n == 0:
            ssq[...], kacc[...], vacc[...], qacc[...] = square, key_part, value_part, query_part
        else:
            ssq[...] += square
            kacc[...] += key_part
            vacc[...] += value_part
            qacc[...] += query_part

    scale = lax.rsqrt(jnp.sum(ssq[...], axis=-1, keepdims=True) * (1.0 / D) + EPSILON)
    rinv[...] = jnp.broadcast_to(scale, (2 * ROWS, LANE)).reshape(2, ROWS, LANE)
    keys = kacc[...] * scale
    keys = (keys * rms_of(keys)).astype(BF16)
    values = (vacc[...] * scale).astype(BF16)
    half = ROWS // 2
    for m in range(2):
        value = values[m * ROWS : (m + 1) * ROWS]
        kvs[m, :ROWS] = keys[m * ROWS : (m + 1) * ROWS]
        kvs[m, ROWS : 2 * ROWS] = value[:, :LANE]
        kvs[m, 2 * ROWS :] = jnp.concatenate([value[:half, LANE:], value[half:, LANE:]], axis=1)

    def kv_copy(j, source, slot, device):
        return pltpu.make_async_remote_copy(
            src_ref=source, dst_ref=kvbuf.at[slot], send_sem=d_send.at[j],
            recv_sem=d_recv.at[j], device_id=device, device_id_type=MESH,
        )

    def relay(j, source):
        return pltpu.make_async_remote_copy(
            src_ref=source, dst_ref=kvbuf.at[2 * j + 1], send_sem=r_send.at[j],
            recv_sem=r_recv.at[j], device_id=sib, device_id_type=MESH,
        )

    direct = [
        kv_copy(0, kvs.at[other], 2, near),
        kv_copy(1, kvs.at[g], 4, ahead),
        kv_copy(2, kvbuf.at[2], 6, behind),
    ]
    direct[0].start()
    direct[1].start()
    relays = [relay(0, kvs.at[g])] + [relay(j, kvbuf.at[2 * j]) for j in range(1, 4)]
    relays[0].start()
    kvbuf[0] = kvs[g]

    row_scale = rinv[g]
    for i in range(4):
        query = qacc[:, i * KEY : (i + 1) * KEY] * row_scale
        q4[i] = (query * rms_of(query)).astype(BF16)
    q_copy = pltpu.make_async_remote_copy(
        src_ref=q4.at[pl.ds(2 * (1 - c), 2)], dst_ref=qall.at[:, 1], send_sem=q_send,
        recv_sem=q_recv, device_id=sib, device_id_type=MESH,
    )
    q_copy.start()
    qall[:, 0] = q4[pl.ds(2 * c, 2)]

    pl.semaphore_wait(met2, 4)
    signal(met3, [sib, z_peer(2), z_peer(Z - 2)])

    direct[0].wait_recv()
    direct[2].start()
    relays[1].start()

    cot_copy.wait()
    for k in range(6):
        wide = cotv[:, :, :, k * LANE : (k + 1) * LANE].astype(F32).reshape(4 * ROWS, LANE)
        turned = jnp.transpose(wide).reshape(8, 2, S, 4 * ROWS)
        turned = jnp.where(g == 0, turned[:, 0], turned[:, 1])
        cott[k * 64 : (k + 1) * 64] = turned.reshape(64, 4 * ROWS).astype(BF16)

    ones = jnp.ones((half, 2 * LANE - VAL), BF16)

    def group(j):
        key = kvbuf[2 * j : 2 * j + 2, :ROWS].reshape(2 * ROWS, KEY)
        head = kvbuf[2 * j : 2 * j + 2, ROWS : 2 * ROWS].reshape(2 * ROWS, LANE)
        tails = []
        for i in range(2):
            tail = kvbuf[2 * j + i, 2 * ROWS :]
            tails.append(jnp.concatenate([tail[:, : VAL - LANE], ones], axis=1))
            tails.append(jnp.concatenate([tail[:, VAL - LANE :], ones], axis=1))
        return key, jnp.concatenate([head, jnp.concatenate(tails, axis=0)], axis=1)

    def attend(query, key, value):
        scores = lax.dot_general(
            query, key, (((1,), (1,)), ((), ())), preferred_element_type=F32
        )
        weights = jnp.exp2(scores * EXP2_SCALE).astype(BF16)
        return jnp.dot(weights, value, preferred_element_type=F32)

    q_copy.wait_recv()
    relays[0].wait_recv()
    query = qall[...].reshape(4 * ROWS, KEY)
    acc[...] = attend(query, *group(0))
    direct[1].wait_recv()
    relays[2].start()
    relays[1].wait_recv()
    acc[...] += attend(query, *group(1))
    direct[2].wait_recv()
    relays[3].start()
    relays[2].wait_recv()
    acc[...] += attend(query, *group(2))
    relays[3].wait_recv()
    last = group(3)

    def att_copy(i):
        return pltpu.make_async_remote_copy(
            src_ref=attx.at[i], dst_ref=attx.at[2 + i], send_sem=a_send.at[i],
            recv_sem=a_recv.at[i], device_id=partner, device_id_type=MESH,
        )

    for i in range(2):
        heads = []
        for j in range(2):
            at = (j * 2 + i) * ROWS
            total = acc[at : at + ROWS] + attend(qall[j, i], *last)
            heads.append(total[:, :VAL] / total[:, VAL : VAL + 1])
        attx[i] = jnp.concatenate(heads, axis=1).astype(BF16)
        att_copy(i).start()
    for i in range(2):
        att_copy(i).wait_recv()

    def p1_copy(d):
        return pltpu.make_async_remote_copy(
            src_ref=psend.at[d], dst_ref=p1r.at[d], send_sem=p1_send.at[d],
            recv_sem=p1_recv.at[d], device_id=x_peer(d), device_id_type=MESH,
        )

    def share(d):
        rows = pl.ds(pl.multiple_of(lax.rem(x + d, X) * ROWS, ROWS), ROWS)
        return jnp.dot(
            cott[rows, :], attx[...].reshape(4 * ROWS, 2 * VAL), preferred_element_type=F32
        )

    for d in (2, 1, 3):
        psend[d] = share(d).astype(BF16)
        p1_copy(d).start()
    total = share(0)
    pl.semaphore_wait(met3, 3)
    for d in (1, 3, 2):
        p1_copy(d).wait_recv()
        total = total + p1r[d].astype(F32)

    for k in range(3):
        red1[k, : Z * S, :] = total[:, k * LANE : (k + 1) * LANE]
        red1[k, Z * S :, :] = jnp.zeros((S * 16 - Z * S, LANE), F32)
    for i in range(S):
        for k in range(3):
            p2s[i, :, k * LANE : (k + 1) * LANE] = red1[k, pl.ds(i, 16, stride=S), :].astype(BF16)

    def p2_copy(d):
        return pltpu.make_async_remote_copy(
            src_ref=p2s.at[lax.rem(s + d, S)], dst_ref=p2r.at[d], send_sem=p2_send.at[d],
            recv_sem=p2_recv.at[d], device_id=s_peer(d), device_id_type=MESH,
        )

    for d in (4, 3, 5, 2, 6, 1, 7):
        p2_copy(d).start()
    mine, theirs = p2s[s].astype(F32), None
    for d in (1, 7, 2, 6, 3, 5, 4):
        p2_copy(d).wait_recv()
        block = p2r[d].astype(F32)
        if d % 2 == 0:
            mine = mine + block
        else:
            theirs = block if theirs is None else theirs + block

    for i in range(Z):
        p3s[c, i] = mine[i : i + 1]
        p3s[1 - c, i] = theirs[i : i + 1]

    def p3_copy(d):
        return pltpu.make_async_remote_copy(
            src_ref=p3s.at[:, lax.rem(z + d, Z)], dst_ref=p3r.at[d], send_sem=p3_send.at[d],
            recv_sem=p3_recv.at[d], device_id=z_peer(d), device_id_type=MESH,
        )

    for d in (6, 5, 7, 4, 8, 3, 9, 2, 10, 1, 11):
        p3_copy(d).start()
    row = p3s[:, z]
    for d in (1, 11, 2, 10, 3, 9, 4, 8, 5, 7, 6):
        p3_copy(d).wait_recv()
        row = row + p3r[d]
    row = row * norm
    grad_out[:, : 2 * VAL] = row[0]
    grad_out[:, 2 * VAL :] = row[1]

    cols = pl.ds(0, COL)
    for n in range(D // COL):
        pltpu.make_async_copy(enc.at[n], enc_out.at[0, :, :, cols], enc_sem.at[n]).wait()
    for copy in direct + relays + [q_copy, att_copy(0), att_copy(1)]:
        copy.wait_send()
    for d in range(1, X):
        p1_copy(d).wait_send()
    for d in range(1, S):
        p2_copy(d).wait_send()
    for d in range(1, Z):
        p3_copy(d).wait_send()


def per_device(dna, dw, pw, qw, kw, vw, cot):
    norm = 1.0 / math.sqrt(X * Z * dna.shape[1])
    dma = pltpu.SemaphoreType.DMA
    vmem = pltpu.VMEM
    hbm = pl.BlockSpec(memory_space=pltpu.MemorySpace.HBM)
    return pl.pallas_call(
        functools.partial(kernel, norm),
        out_shape=(
            jax.ShapeDtypeStruct((1, 2, ROWS, D), BF16),
            jax.ShapeDtypeStruct((1, 4 * VAL), F32),
        ),
        in_specs=[hbm] * 7,
        out_specs=(hbm, pl.BlockSpec(memory_space=pltpu.VMEM)),
        scratch_shapes=[
            vmem((2, 2 * ROWS, C_IN), BF16),
            vmem((3, C_IN), BF16),
            vmem((C_IN, D), BF16),
            vmem((D, 4 * KEY), BF16),
            vmem((D, KEY), BF16),
            vmem((VAL, D), BF16),
            vmem((2, 2, ROWS, C_IN), BF16),
            vmem((6, 2 * ROWS, LANE), F32),
            vmem((12, ROWS + 16, LANE), F32),
            vmem((2 * ROWS, C_IN), BF16),
            vmem((D // COL, 2, ROWS, COL), BF16),
            vmem((2 * ROWS, LANE), F32),
            vmem((2, ROWS, LANE), F32),
            vmem((ROWS, 4 * KEY), F32),
            vmem((2 * ROWS, KEY), F32),
            vmem((2 * ROWS, VAL), F32),
            vmem((2, 12, 1, LANE), F32),
            vmem((2, 12, 1, LANE), F32),
            vmem((4, ROWS, KEY), BF16),
            vmem((2, 2, ROWS, KEY), BF16),
            vmem((2, KV_ROWS, LANE), BF16),
            vmem((8, KV_ROWS, LANE), BF16),
            vmem((4 * ROWS, 2 * LANE), F32),
            vmem((X * ROWS, 4 * ROWS), BF16),
            vmem((4, ROWS, 2 * VAL), BF16),
            vmem((X, ROWS, 2 * VAL), BF16),
            vmem((X, ROWS, 2 * VAL), BF16),
            vmem((3, 16 * S, LANE), F32),
            vmem((S, 16, 2 * VAL), BF16),
            vmem((S, 16, 2 * VAL), BF16),
            vmem((2, Z, 1, 2 * VAL), F32),
            vmem((Z, 2, 1, 2 * VAL), F32),
            dma((8,)), dma((D // COL,)), dma((2,)), dma((2,)), dma, dma, dma, dma,
            dma((3,)), dma((3,)), dma((4,)), dma((4,)), dma((2,)), dma((2,)),
            dma((X,)), dma((X,)), dma((S,)), dma((S,)), dma((Z,)), dma((Z,)),
            pltpu.SemaphoreType.REGULAR, pltpu.SemaphoreType.REGULAR, pltpu.SemaphoreType.REGULAR,
        ],
        compiler_params=pltpu.CompilerParams(
            collective_id=0, has_side_effects=True, vmem_limit_bytes=62 * 2**20
        ),
        name="window_step",
    )(dna, dw, pw, qw, kw, vw.T, cot)


def solution(mesh):
    rows = P("batch", None, "seq", None)
    return jax.shard_map(
        per_device,
        mesh=mesh,
        in_specs=(rows, P(), P(), P(), P(), P(), rows),
        out_specs=(rows, P(("batch", "segment", "seq"), None)),
        check_vma=False,
    )
```

time: 68.9 us -> 56.8 us (0.82)
  local copies, waits for them, and re-layouts: 9.51 us -> 3.17 us
  Pallas kernels: 58.4 us -> 52.8 us
    unnamed x15 -> x2, local copies, waits for them, and re-layouts: 9.51 us -> 3.17 us
    pallas_call x1, Pallas kernels: 58.4 us -> 52.8 us  [per_device(): pl.pallas_call(functools.partial(kernel, norm), out_shape=(jax.ShapeDtype...]
where the time goes in v2:
time: 56.8 us; the launch traced here: 56.6 us
  Pallas kernels  52.8 us (93%)
  local copies, waits for them, and re-layouts  3.17 us (6%)
  between operations  0.64 us (1%)
    pallas_call x1, Pallas kernels, per_device(): pl.pallas_call(functools.partial(kernel, norm), out_shape=(jax.ShapeDtype...  52.8 us
    unnamed x2, local copies, waits for them, and re-layouts  3.17 us

profile of v2, /device:TPU:1, one launch (start us, length us, event | category | flops | bytes accessed | tf_op | source)
XLA Modules:
  0.0 56.6 jit_solution(1045170256626111345)
XLA Ops:
  0.6 52.8 %window_step.1 = (bf16[1,2,96,1536]{3,2,1,0:T(8,128)(2,1)}, f32[1,768]{1,0:T(1,128)}) custom-call(bf16[1,2,192,768]{3,2,1,0:T(8,128)(2,1)} %dna.1, bf16[3,768]{1,0:T(4,128)(2,1)} %dw.1, bf16[768,1536]{1,0:T(8,128)(2,1)} %pw.1, bf16[1536,512]{1,0:T(8,128)(2,1)} %qw.1, bf16[1536,128]{1,0:T(8,128)(2,1)} %kw.1, bf16[192,1536]{1,0:T(8,128)(2,1)} %bitcast.1, ...), custom_call_target="tpu_custom_call" | custom-call | tf_op jit(solution)/shard_map/window_step/pallas_call | solution.py:357
  53.5 1.9 %copy.11 = bf16[1,2,96,1536]{3,2,1,0:T(8,128)(2,1)} copy(bf16[1,2,96,1536]{3,2,1,0:T(8,128)(2,1)} %get-tuple-element.4) | data formatting | bytes 1179648
  55.4 1.3 %copy.12 = f32[1,768]{1,0:T(1,128)} copy(f32[1,768]{1,0:T(1,128)} %get-tuple-element.5) | data formatting | bytes 6144

commit v3 on v2

v3 whole, which is shorter than its diff:
```python
import functools
import math

import jax
import jax.numpy as jnp
from jax import lax
from jax.experimental import pallas as pl
from jax.experimental.pallas import tpu as pltpu
from jax.sharding import PartitionSpec as P

MESH = pl.DeviceIdType.MESH
F32 = jnp.float32
BF16 = jnp.bfloat16

C_IN = 768
D = 1536
KEY = 128
VAL = 192
ROWS = 96
X, Z, S = 4, 12, 8
EPSILON = 1e-06
LANE = 128
COL = 256
KV_ROWS = 2 * ROWS + ROWS // 2
EXP2_SCALE = math.log2(math.e) / math.sqrt(KEY)


def gelu(u):
    inner = math.sqrt(2.0 / math.pi) * (u + 0.044715 * (u * u * u))
    return 0.5 * u * (1.0 + jnp.tanh(inner))


def rms_of(values):
    return lax.rsqrt(jnp.mean(values * values, axis=-1, keepdims=True) + EPSILON)


def kernel(
    norm,
    dna, dw, pw, qw, kw, vw, cot,
    enc_out, grad_out,
    xin, dwv, pwv, qwv, kwv, vwv, cotv,
    xf, ext, pooled, edge, enc,
    hs, hr, q4, qall, kvs, kvbuf, acc, cott, attx, own, psend, p1r, red1, p2s, p2r, p3s, p3r,
    in_sem, enc_sem, h_send, h_recv, cot_send, cot_recv, q_send, q_recv,
    d_send, d_recv, r_send, r_recv, a_send, a_recv,
    p1_send, p1_recv, p2_send, p2_recv, p3_send, p3_recv, met1, met2, met3,
):
    b, g, s = lax.axis_index("batch"), lax.axis_index("segment"), lax.axis_index("seq")
    x, z = b // Z, lax.rem(b, Z)
    h, c = s // 2, lax.rem(s, 2)
    other = 1 - g
    sign = 2 * g - 1

    def x_peer(d):
        return (lax.rem(x + d, X) * Z + z, g, s)

    def s_peer(d):
        return (b, g, lax.rem(s + d, S))

    def z_peer(d):
        return (x * Z + lax.rem(z + d, Z), g, s)

    sib = (b, g, h * 2 + (1 - c))
    partner = (b, other, s)
    near = (b, other, lax.rem(h + sign + 4, 4) * 2 + c)
    ahead = (b, g, lax.rem(h + sign + 4, 4) * 2 + c)
    behind = (b, g, lax.rem(h - sign + 4, 4) * 2 + c)
    cross = (b, g, lax.rem(s + 2 * c - 1 + S, S))

    def signal(semaphore, devices):
        for device in devices:
            pl.semaphore_signal(semaphore, inc=1, device_id=device, device_id_type=MESH)

    barrier = pltpu.get_barrier_semaphore()
    beside = [partner, near, x_peer(1), x_peer(X - 1), z_peer(1), z_peer(Z - 1)]
    signal(barrier, [cross, sib] + beside)

    loads = [
        pltpu.make_async_copy(dna.at[0], xin, in_sem.at[0]),
        pltpu.make_async_copy(dw, dwv, in_sem.at[1]),
        pltpu.make_async_copy(pw, pwv, in_sem.at[2]),
        pltpu.make_async_copy(kw, kwv, in_sem.at[3]),
        pltpu.make_async_copy(vw, vwv, in_sem.at[4]),
        pltpu.make_async_copy(qw, qwv, in_sem.at[5]),
        pltpu.make_async_copy(cot.at[0, g], cotv.at[0, 0], in_sem.at[6]),
        pltpu.make_async_copy(cot.at[0, other], cotv.at[1, 0], in_sem.at[7]),
    ]
    for load in loads:
        load.start()

    loads[0].wait()
    for m in range(2):
        for k in range(6):
            i = m * 6 + k
            xf[k] = xin[m, :, k * LANE : (k + 1) * LANE].astype(F32)
            even = xf[k, pl.ds(0, ROWS, stride=2), :]
            ext[i, 7:8, :] = jnp.zeros((1, LANE), F32)
            ext[i, 8 : 8 + ROWS, :] = even
            ext[i, 8 + ROWS : 9 + ROWS, :] = jnp.zeros((1, LANE), F32)
            hs[0, i] = even[0:1]
            hs[1, i] = even[ROWS - 1 : ROWS]

    pl.semaphore_wait(barrier, 8)
    to_left = pltpu.make_async_remote_copy(
        src_ref=hs.at[0], dst_ref=hr.at[1], send_sem=h_send.at[0], recv_sem=h_recv.at[1],
        device_id=s_peer(S - 1), device_id_type=MESH,
    )
    to_right = pltpu.make_async_remote_copy(
        src_ref=hs.at[1], dst_ref=hr.at[0], send_sem=h_send.at[1], recv_sem=h_recv.at[0],
        device_id=s_peer(1), device_id_type=MESH,
    )
    to_left.start()
    to_right.start()
    signal(met1, beside)
    loads[1].wait()
    w = dwv[...].astype(F32)
    for m in range(2):
        for k in range(6):
            i = m * 6 + k
            part = slice(k * LANE, (k + 1) * LANE)
            total = w[0:1, part] * ext[i, 7 : 7 + ROWS, :]
            total = total + w[1:2, part] * ext[i, 8 : 8 + ROWS, :]
            total = total + w[2:3, part] * ext[i, 9 : 9 + ROWS, :]
            pooled[m * ROWS : (m + 1) * ROWS, part] = total.astype(BF16)
    loads[2].wait()
    for n in range(D // COL):
        cols = slice(n * COL, (n + 1) * COL)
        u = jnp.dot(pooled[...], pwv[:, cols], preferred_element_type=F32)
        enc[n] = gelu(u).astype(BF16).reshape(2, ROWS, COL)

    pl.semaphore_wait(met1, 6)
    signal(met2, [ahead, behind, z_peer(2), z_peer(Z - 2)])
    loads[6].wait()
    loads[7].wait()
    cot_copy = pltpu.make_async_remote_copy(
        src_ref=cotv.at[:, 0], dst_ref=cotv.at[:, 1], send_sem=cot_send, recv_sem=cot_recv,
        device_id=sib, device_id_type=MESH,
    )
    cot_copy.start()

    to_left.wait()
    to_right.wait()
    edge[...] = jnp.zeros_like(edge)
    for m in range(2):
        for k in range(6):
            i = m * 6 + k
            part = slice(k * LANE, (k + 1) * LANE)
            before = jnp.where(s > 0, hr[0, i], 0.0)
            after = jnp.where(s < S - 1, hr[1, i], 0.0)
            total = w[0:1, part] * before + w[1:2, part] * ext[i, 8:9, :]
            edge[2 * m : 2 * m + 1, part] = total + w[2:3, part] * ext[i, 9:10, :]
            end = 7 + ROWS
            total = w[0:1, part] * ext[i, end - 1 : end, :] + w[1:2, part] * ext[i, end : end + 1, :]
            edge[2 * m + 1 : 2 * m + 2, part] = total + w[2:3, part] * after
    edge_rows = edge[...].astype(BF16)
    row = lax.broadcasted_iota(jnp.int32, (16, COL), 0)
    for n in range(D // COL):
        cols = slice(n * COL, (n + 1) * COL)
        u = gelu(jnp.dot(edge_rows, pwv[:, cols], preferred_element_type=F32))
        for m in range(2):
            first = jnp.where(row == 0, u[2 * m : 2 * m + 1], enc[n, m, :16].astype(F32))
            enc[n, m, :16] = first.astype(BF16)
            final = jnp.where(row == 15, u[2 * m + 1 : 2 * m + 2], enc[n, m, ROWS - 16 :].astype(F32))
            enc[n, m, ROWS - 16 :] = final.astype(BF16)
        pltpu.make_async_copy(enc.at[n], enc_out.at[0, :, :, cols], enc_sem.at[n]).start()

    for load in loads[3:6]:
        load.wait()
    half = ROWS // 2

    def rows_of(micro):
        rows = jnp.concatenate([enc[n, micro] for n in range(D // COL)], axis=1)
        total = jnp.zeros((ROWS, LANE), F32)
        for n in range(D // LANE):
            wide = rows[:, n * LANE : (n + 1) * LANE].astype(F32)
            total = total + wide * wide
        return rows, lax.rsqrt(jnp.sum(total, axis=-1, keepdims=True) * (1.0 / D) + EPSILON)

    def project(micro):
        rows, scale = rows_of(micro)
        key = jnp.dot(rows, kwv[...], preferred_element_type=F32) * scale
        value = lax.dot_general(
            rows, vwv[...], (((1,), (1,)), ((), ())), preferred_element_type=F32
        )
        value = (value * scale).astype(BF16)
        kvs[micro, :ROWS] = (key * rms_of(key)).astype(BF16)
        kvs[micro, ROWS : 2 * ROWS] = value[:, :LANE]
        kvs[micro, 2 * ROWS :] = jnp.concatenate([value[:half, LANE:], value[half:, LANE:]], axis=1)
        return rows, scale

    def kv_copy(j, source, slot, device, part=slice(None)):
        return pltpu.make_async_remote_copy(
            src_ref=source.at[part], dst_ref=kvbuf.at[slot, part], send_sem=d_send.at[j],
            recv_sem=d_recv.at[j], device_id=device, device_id_type=MESH,
        )

    def relay(j, source):
        return pltpu.make_async_remote_copy(
            src_ref=source, dst_ref=kvbuf.at[2 * j + 1], send_sem=r_send.at[j],
            recv_sem=r_recv.at[j], device_id=sib, device_id_type=MESH,
        )

    parts = (pl.ds(0, 112), pl.ds(112, KV_ROWS - 112))
    to_near = [kv_copy(j, kvs.at[other], 2, near, part) for j, part in enumerate(parts)]
    forward = [kv_copy(2 + j, kvbuf.at[2], 6, behind, part) for j, part in enumerate(parts)]
    to_ahead = kv_copy(4, kvs.at[g], 4, ahead)
    project(other)
    to_near[0].start()
    to_near[1].start()
    rows, scale = project(g)
    to_ahead.start()
    relays = [relay(0, kvs.at[g])] + [relay(j, kvbuf.at[2 * j]) for j in range(1, 4)]
    relays[0].start()
    kvbuf[0] = kvs[g]

    queries = jnp.dot(rows, qwv[...], preferred_element_type=F32) * scale
    for i in range(4):
        query = queries[:, i * KEY : (i + 1) * KEY]
        q4[i] = (query * rms_of(query)).astype(BF16)
    q_copy = pltpu.make_async_remote_copy(
        src_ref=q4.at[pl.ds(2 * (1 - c), 2)], dst_ref=qall.at[:, 1], send_sem=q_send,
        recv_sem=q_recv, device_id=sib, device_id_type=MESH,
    )
    q_copy.start()
    qall[:, 0] = q4[pl.ds(2 * c, 2)]

    pl.semaphore_wait(met2, 4)
    signal(met3, [sib, z_peer(2), z_peer(Z - 2)])

    def turn(k):
        wide = cotv[:, :, :, k * LANE : (k + 1) * LANE].astype(F32).reshape(4 * ROWS, LANE)
        turned = jnp.transpose(wide).reshape(8, 2, S, 4 * ROWS)
        turned = jnp.where(g == 0, turned[:, 0], turned[:, 1])
        cott[k * 64 : (k + 1) * 64] = turned.reshape(64, 4 * ROWS).astype(BF16)

    cot_copy.wait()
    for j in range(2):
        to_near[j].wait_recv()
        forward[j].start()
        if j == 1:
            relays[1].start()
        for k in range(3):
            turn(3 * j + k)

    ones = jnp.ones((half, 2 * LANE - VAL), BF16)

    def group(j):
        key = kvbuf[2 * j : 2 * j + 2, :ROWS].reshape(2 * ROWS, KEY)
        head = kvbuf[2 * j : 2 * j + 2, ROWS : 2 * ROWS].reshape(2 * ROWS, LANE)
        tails = []
        for i in range(2):
            tail = kvbuf[2 * j + i, 2 * ROWS :]
            tails.append(jnp.concatenate([tail[:, : VAL - LANE], ones], axis=1))
            tails.append(jnp.concatenate([tail[:, VAL - LANE :], ones], axis=1))
        return key, jnp.concatenate([head, jnp.concatenate(tails, axis=0)], axis=1)

    def attend(query, key, value):
        scores = lax.dot_general(
            query, key, (((1,), (1,)), ((), ())), preferred_element_type=F32
        )
        weights = jnp.exp2(scores * EXP2_SCALE).astype(BF16)
        return jnp.dot(weights, value, preferred_element_type=F32)

    q_copy.wait_recv()
    relays[0].wait_recv()
    query = qall[...].reshape(4 * ROWS, KEY)
    acc[...] = attend(query, *group(0))
    to_ahead.wait_recv()
    relays[2].start()
    relays[1].wait_recv()
    acc[...] += attend(query, *group(1))
    forward[0].wait_recv()
    forward[1].wait_recv()
    relays[3].start()
    relays[2].wait_recv()
    acc[...] += attend(query, *group(2))
    relays[3].wait_recv()
    last = group(3)

    def att_copy(t):
        return pltpu.make_async_remote_copy(
            src_ref=attx.at[t, :2], dst_ref=attx.at[t, 2:], send_sem=a_send.at[t],
            recv_sem=a_recv.at[t], device_id=partner, device_id_type=MESH,
        )

    def head(j, i):
        at = (j * 2 + i) * ROWS
        total = acc[at : at + ROWS] + attend(qall[j, i], *last)
        return (total[:, :VAL] / total[:, VAL : VAL + 1]).astype(BF16)

    low = [head(0, i) for i in range(2)]
    for i in range(2):
        attx[0, i] = low[i][:, :LANE]
    att_copy(0).start()
    high = [head(1, i) for i in range(2)]
    for i in range(2):
        attx[1, i] = jnp.concatenate([low[i][:, LANE:], high[i][:, : 2 * LANE - VAL]], axis=1)
    att_copy(1).start()
    for i in range(2):
        attx[2, i] = high[i][:, 2 * LANE - VAL :]
    att_copy(2).start()

    def share(t, first):
        part = cott[:, : 2 * ROWS] if first else cott[:, 2 * ROWS :]
        pair = attx[t, :2] if first else attx[t, 2:]
        part = jnp.dot(part, pair.reshape(2 * ROWS, LANE), preferred_element_type=F32)
        return part.reshape(X, ROWS, LANE)

    def p1_copy(t, d):
        return pltpu.make_async_remote_copy(
            src_ref=psend.at[t, lax.rem(x + d, X)], dst_ref=p1r.at[t, d],
            send_sem=p1_send.at[t, d], recv_sem=p1_recv.at[t, d],
            device_id=x_peer(d), device_id_type=MESH,
        )

    for t in range(3):
        own[t] = share(t, True)
    for t in range(3):
        att_copy(t).wait_recv()
        full = own[t] + share(t, False)
        own[t] = full
        psend[t] = full.astype(BF16)
        for d in (2, 1, 3):
            p1_copy(t, d).start()

    def p2_copy(t, d):
        return pltpu.make_async_remote_copy(
            src_ref=p2s.at[t, lax.rem(s + d, S)], dst_ref=p2r.at[t, d],
            send_sem=p2_send.at[t, d], recv_sem=p2_recv.at[t, d],
            device_id=s_peer(d), device_id_type=MESH,
        )

    pl.semaphore_wait(met3, 3)
    for t in range(3):
        total = own[t, x]
        for d in (1, 3, 2):
            p1_copy(t, d).wait_recv()
            total = total + p1r[t, d].astype(F32)
        red1[t, : Z * S, :] = total
        red1[t, Z * S :, :] = jnp.zeros((S * 16 - Z * S, LANE), F32)
        for i in range(S):
            p2s[t, i] = red1[t, pl.ds(i, 16, stride=S), :].astype(BF16)
        for d in (4, 3, 5, 2, 6, 1, 7):
            p2_copy(t, d).start()

    for t in range(3):
        mine, theirs = p2s[t, s].astype(F32), None
        for d in (1, 7, 2, 6, 3, 5, 4):
            p2_copy(t, d).wait_recv()
            block = p2r[t, d].astype(F32)
            if d % 2 == 0:
                mine = mine + block
            else:
                theirs = block if theirs is None else theirs + block
        part = slice(t * LANE, (t + 1) * LANE)
        for i in range(Z):
            p3s[c, i, :, part] = mine[i : i + 1]
            p3s[1 - c, i, :, part] = theirs[i : i + 1]

    def p3_copy(d):
        return pltpu.make_async_remote_copy(
            src_ref=p3s.at[:, lax.rem(z + d, Z)], dst_ref=p3r.at[d], send_sem=p3_send.at[d],
            recv_sem=p3_recv.at[d], device_id=z_peer(d), device_id_type=MESH,
        )

    for d in (6, 5, 7, 4, 8, 3, 9, 2, 10, 1, 11):
        p3_copy(d).start()
    row = p3s[:, z]
    for d in (1, 11, 2, 10, 3, 9, 4, 8, 5, 7, 6):
        p3_copy(d).wait_recv()
        row = row + p3r[d]
    row = row * norm
    grad_out[:, : 2 * VAL] = row[0]
    grad_out[:, 2 * VAL :] = row[1]

    cols = pl.ds(0, COL)
    for n in range(D // COL):
        pltpu.make_async_copy(enc.at[n], enc_out.at[0, :, :, cols], enc_sem.at[n]).wait()
    for copy in to_near + forward + [to_ahead] + relays + [q_copy]:
        copy.wait_send()
    for t in range(3):
        att_copy(t).wait_send()
        for d in range(1, X):
            p1_copy(t, d).wait_send()
        for d in range(1, S):
            p2_copy(t, d).wait_send()
    for d in range(1, Z):
        p3_copy(d).wait_send()


def deliver(encoded, grad, encoded_out, grad_out, rows, line, load_sem, store_sem):
    half = ROWS // 2
    places = []
    for i in range(4):
        at = (i // 2, pl.ds(i % 2 * half, half))
        places.append((encoded.at[0, *at], rows.at[at], encoded_out.at[0, *at]))
    places.append((grad, line, grad_out))
    loads = [
        pltpu.make_async_copy(source, held, load_sem.at[i])
        for i, (source, held, _) in enumerate(places)
    ]
    stores = [
        pltpu.make_async_copy(held, target, store_sem.at[i])
        for i, (_, held, target) in enumerate(places)
    ]
    for load in loads:
        load.start()
    for load, store in zip(loads, stores):
        load.wait()
        store.start()
    for store in stores:
        store.wait()


def per_device(dna, dw, pw, qw, kw, vw, cot):
    norm = 1.0 / math.sqrt(X * Z * dna.shape[1])
    dma = pltpu.SemaphoreType.DMA
    vmem = pltpu.VMEM
    hbm = pl.BlockSpec(memory_space=pltpu.MemorySpace.HBM)
    encoded, grad = pl.pallas_call(
        functools.partial(kernel, norm),
        out_shape=(
            jax.ShapeDtypeStruct((1, 2, ROWS, D), BF16),
            jax.ShapeDtypeStruct((1, 4 * VAL), F32),
        ),
        in_specs=[hbm] * 7,
        out_specs=(hbm, pl.BlockSpec(memory_space=pltpu.VMEM)),
        scratch_shapes=[
            vmem((2, 2 * ROWS, C_IN), BF16),
            vmem((3, C_IN), BF16),
            vmem((C_IN, D), BF16),
            vmem((D, 4 * KEY), BF16),
            vmem((D, KEY), BF16),
            vmem((VAL, D), BF16),
            vmem((2, 2, ROWS, C_IN), BF16),
            vmem((6, 2 * ROWS, LANE), F32),
            vmem((12, ROWS + 16, LANE), F32),
            vmem((2 * ROWS, C_IN), BF16),
            vmem((16, C_IN), F32),
            vmem((D // COL, 2, ROWS, COL), BF16),
            vmem((2, 12, 1, LANE), F32),
            vmem((2, 12, 1, LANE), F32),
            vmem((4, ROWS, KEY), BF16),
            vmem((2, 2, ROWS, KEY), BF16),
            vmem((2, KV_ROWS, LANE), BF16),
            vmem((8, KV_ROWS, LANE), BF16),
            vmem((4 * ROWS, 2 * LANE), F32),
            vmem((X * ROWS, 4 * ROWS), BF16),
            vmem((3, 4, ROWS, LANE), BF16),
            vmem((3, X, ROWS, LANE), F32),
            vmem((3, X, ROWS, LANE), BF16),
            vmem((3, X, ROWS, LANE), BF16),
            vmem((3, 16 * S, LANE), F32),
            vmem((3, S, 16, LANE), BF16),
            vmem((3, S, 16, LANE), BF16),
            vmem((2, Z, 1, 2 * VAL), F32),
            vmem((Z, 2, 1, 2 * VAL), F32),
            dma((8,)), dma((D // COL,)), dma((2,)), dma((2,)), dma, dma, dma, dma,
            dma((5,)), dma((5,)), dma((4,)), dma((4,)), dma((3,)), dma((3,)),
            dma((3, X)), dma((3, X)), dma((3, S)), dma((3, S)), dma((Z,)), dma((Z,)),
            pltpu.SemaphoreType.REGULAR, pltpu.SemaphoreType.REGULAR, pltpu.SemaphoreType.REGULAR,
        ],
        compiler_params=pltpu.CompilerParams(
            collective_id=0, has_side_effects=True, vmem_limit_bytes=62 * 2**20
        ),
        name="window_step",
    )(dna, dw, pw, qw, kw, vw.T, cot)
    return pl.pallas_call(
        deliver,
        out_shape=(
            jax.ShapeDtypeStruct(encoded.shape, BF16),
            jax.ShapeDtypeStruct(grad.shape, F32),
        ),
        in_specs=[hbm] * 2,
        out_specs=(hbm, hbm),
        scratch_shapes=[
            vmem((2, ROWS, D), BF16), vmem((1, 4 * VAL), F32), dma((5,)), dma((5,)),
        ],
        compiler_params=pltpu.CompilerParams(vmem_limit_bytes=62 * 2**20),
        name="deliver",
    )(encoded, grad)


def solution(mesh):
    rows = P("batch", None, "seq", None)
    return jax.shard_map(
        per_device,
        mesh=mesh,
        in_specs=(rows, P(), P(), P(), P(), P(), rows),
        out_specs=(rows, P(("batch", "segment", "seq"), None)),
        check_vma=False,
    )
```

time: 56.8 us -> 52.6 us (0.926)
  local copies, waits for them, and re-layouts: 3.17 us -> 0 us
  Pallas kernels: 52.8 us -> 51.8 us
    unnamed x2 -> x0, local copies, waits for them, and re-layouts: 3.17 us -> none
    pallas_call x1, Pallas kernels: 52.8 us -> 50 us  [per_device(): pl.pallas_call(functools.partial(kernel, norm), out_shape=(jax.ShapeDtype...]
    pallas_call x0 -> x1, Pallas kernels: none -> 1.87 us  [per_device(): pl.pallas_call(deliver, out_shape=(jax.ShapeDtypeStruct(encoded.shape, BF...]
where the time goes in v3:
time: 52.6 us; the launch traced here: 52.5 us
  Pallas kernels  51.8 us (98%)
  between operations  0.64 us (1%)
    pallas_call x1, Pallas kernels, per_device(): pl.pallas_call(functools.partial(kernel, norm), out_shape=(jax.ShapeDtype...  50 us
    pallas_call x1, Pallas kernels, per_device(): pl.pallas_call(deliver, out_shape=(jax.ShapeDtypeStruct(encoded.shape, BF...  1.87 us

profile of v3, /device:TPU:1, one launch (start us, length us, event | category | flops | bytes accessed | tf_op | source)
XLA Modules:
  0.0 52.5 jit_solution(4072777574232566359)
XLA Ops:
  0.6 50.0 %window_step.1 = (bf16[1,2,96,1536]{3,2,1,0:T(8,128)(2,1)}, f32[1,768]{1,0:T(1,128)}) custom-call(bf16[1,2,192,768]{3,2,1,0:T(8,128)(2,1)} %dna.1, bf16[3,768]{1,0:T(4,128)(2,1)} %dw.1, bf16[768,1536]{1,0:T(8,128)(2,1)} %pw.1, bf16[1536,512]{1,0:T(8,128)(2,1)} %qw.1, bf16[1536,128]{1,0:T(8,128)(2,1)} %kw.1, bf16[192,1536]{1,0:T(8,128)(2,1)} %bitcast.1, ...), custom_call_target="tpu_custom_call" | custom-call | tf_op jit(solution)/shard_map/window_step/pallas_call | solution.py:420
  50.6 1.9 %deliver.1 = (bf16[1,2,96,1536]{3,2,1,0:T(8,128)(2,1)}, f32[1,768]{1,0:T(1,128)}) custom-call(bf16[1,2,96,1536]{3,2,1,0:T(8,128)(2,1)} %get-tuple-element.4.encoded, f32[1,768]{1,0:T(1,128)} %get-tuple-element.5.grad), custom_call_target="tpu_custom_call" | custom-call | tf_op jit(solution)/shard_map/deliver/pallas_call | solution.py:468

commit v4 on v3

--- a/solution.py
+++ b/solution.py
@@ -38,7 +38,7 @@
     norm,
     dna, dw, pw, qw, kw, vw, cot,
     enc_out, grad_out,
-    xin, dwv, pwv, qwv, kwv, vwv, cotv,
+    ein, xin, dwv, pwv, qwv, kwv, vwv, cotv,
     xf, ext, pooled, edge, enc,
     hs, hr, q4, qall, kvs, kvbuf, acc, cott, attx, own, psend, p1r, red1, p2s, p2r, p3s, p3r,
     in_sem, enc_sem, h_send, h_recv, cot_send, cot_recv, q_send, q_recv,
@@ -75,6 +75,10 @@
     beside = [partner, near, x_peer(1), x_peer(X - 1), z_peer(1), z_peer(Z - 1)]
     signal(barrier, [cross, sib] + beside)
 
+    ends = [
+        pltpu.make_async_copy(dna.at[0, :, pl.ds(0, 16)], ein.at[0], in_sem.at[8]),
+        pltpu.make_async_copy(dna.at[0, :, pl.ds(2 * ROWS - 16, 16)], ein.at[1], in_sem.at[9]),
+    ]
     loads = [
         pltpu.make_async_copy(dna.at[0], xin, in_sem.at[0]),
         pltpu.make_async_copy(dw, dwv, in_sem.at[1]),
@@ -85,20 +89,16 @@
         pltpu.make_async_copy(cot.at[0, g], cotv.at[0, 0], in_sem.at[6]),
         pltpu.make_async_copy(cot.at[0, other], cotv.at[1, 0], in_sem.at[7]),
     ]
-    for load in loads:
+    for load in ends + loads:
         load.start()
 
-    loads[0].wait()
+    ends[0].wait()
+    ends[1].wait()
     for m in range(2):
         for k in range(6):
-            i = m * 6 + k
-            xf[k] = xin[m, :, k * LANE : (k + 1) * LANE].astype(F32)
-            even = xf[k, pl.ds(0, ROWS, stride=2), :]
-            ext[i, 7:8, :] = jnp.zeros((1, LANE), F32)
-            ext[i, 8 : 8 + ROWS, :] = even
-            ext[i, 8 + ROWS : 9 + ROWS, :] = jnp.zeros((1, LANE), F32)
-            hs[0, i] = even[0:1]
-            hs[1, i] = even[ROWS - 1 : ROWS]
+            part = slice(k * LANE, (k + 1) * LANE)
+            hs[0, m * 6 + k] = ein[0, m, :, part].astype(F32)[0:1]
+            hs[1, m * 6 + k] = ein[1, m, :, part].astype(F32)[14:15]
 
     pl.semaphore_wait(barrier, 8)
     to_left = pltpu.make_async_remote_copy(
@@ -112,6 +112,16 @@
     to_left.start()
     to_right.start()
     signal(met1, beside)
+
+    loads[0].wait()
+    for m in range(2):
+        for k in range(6):
+            i = m * 6 + k
+            xf[k] = xin[m, :, k * LANE : (k + 1) * LANE].astype(F32)
+            ext[i, 7:8, :] = jnp.zeros((1, LANE), F32)
+            ext[i, 8 : 8 + ROWS, :] = xf[k, pl.ds(0, ROWS, stride=2), :]
+            ext[i, 8 + ROWS : 9 + ROWS, :] = jnp.zeros((1, LANE), F32)
+
     loads[1].wait()
     w = dwv[...].astype(F32)
     for m in range(2):
@@ -200,15 +210,15 @@
             recv_sem=r_recv.at[j], device_id=sib, device_id_type=MESH,
         )
 
-    parts = (pl.ds(0, 112), pl.ds(112, KV_ROWS - 112))
+    parts = [pl.ds(i * 80, 80) for i in range(3)]
     to_near = [kv_copy(j, kvs.at[other], 2, near, part) for j, part in enumerate(parts)]
-    forward = [kv_copy(2 + j, kvbuf.at[2], 6, behind, part) for j, part in enumerate(parts)]
-    to_ahead = kv_copy(4, kvs.at[g], 4, ahead)
+    forward = [kv_copy(3 + j, kvbuf.at[2], 6, behind, part) for j, part in enumerate(parts)]
+    to_ahead = kv_copy(6, kvs.at[g], 4, ahead)
     project(other)
     to_near[0].start()
     to_near[1].start()
+    to_near[2].start()
     rows, scale = project(g)
-    to_ahead.start()
     relays = [relay(0, kvs.at[g])] + [relay(j, kvbuf.at[2 * j]) for j in range(1, 4)]
     relays[0].start()
     kvbuf[0] = kvs[g]
@@ -222,6 +232,7 @@
         recv_sem=q_recv, device_id=sib, device_id_type=MESH,
     )
     q_copy.start()
+    to_ahead.start()
     qall[:, 0] = q4[pl.ds(2 * c, 2)]
 
     pl.semaphore_wait(met2, 4)
@@ -234,13 +245,13 @@
         cott[k * 64 : (k + 1) * 64] = turned.reshape(64, 4 * ROWS).astype(BF16)
 
     cot_copy.wait()
-    for j in range(2):
+    for j in range(3):
         to_near[j].wait_recv()
         forward[j].start()
-        if j == 1:
+        if j == 2:
             relays[1].start()
-        for k in range(3):
-            turn(3 * j + k)
+        for k in range(2):
+            turn(2 * j + k)
 
     ones = jnp.ones((half, 2 * LANE - VAL), BF16)
 
@@ -271,6 +282,7 @@
     acc[...] += attend(query, *group(1))
     forward[0].wait_recv()
     forward[1].wait_recv()
+    forward[2].wait_recv()
     relays[3].start()
     relays[2].wait_recv()
     acc[...] += attend(query, *group(2))
@@ -283,16 +295,18 @@
             recv_sem=a_recv.at[t], device_id=partner, device_id_type=MESH,
         )
 
-    def head(j, i):
-        at = (j * 2 + i) * ROWS
-        total = acc[at : at + ROWS] + attend(qall[j, i], *last)
-        return (total[:, :VAL] / total[:, VAL : VAL + 1]).astype(BF16)
-
-    low = [head(0, i) for i in range(2)]
+    def head(j):
+        at = slice(j * 2 * ROWS, (j + 1) * 2 * ROWS)
+        total = acc[at] + attend(qall[j].reshape(2 * ROWS, KEY), *last)
+        inverse = 1.0 / total[:, VAL : VAL + 1]
+        attended = (total[:, :VAL] * inverse).astype(BF16)
+        return attended[:ROWS], attended[ROWS:]
+
+    low = head(0)
     for i in range(2):
         attx[0, i] = low[i][:, :LANE]
     att_copy(0).start()
-    high = [head(1, i) for i in range(2)]
+    high = head(1)
     for i in range(2):
         attx[1, i] = jnp.concatenate([low[i][:, LANE:], high[i][:, : 2 * LANE - VAL]], axis=1)
     att_copy(1).start()
@@ -426,6 +440,7 @@
         in_specs=[hbm] * 7,
         out_specs=(hbm, pl.BlockSpec(memory_space=pltpu.VMEM)),
         scratch_shapes=[
+            vmem((2, 2, 16, C_IN), BF16),
             vmem((2, 2 * ROWS, C_IN), BF16),
             vmem((3, C_IN), BF16),
             vmem((C_IN, D), BF16),
@@ -455,8 +470,8 @@
             vmem((3, S, 16, LANE), BF16),
             vmem((2, Z, 1, 2 * VAL), F32),
             vmem((Z, 2, 1, 2 * VAL), F32),
-            dma((8,)), dma((D // COL,)), dma((2,)), dma((2,)), dma, dma, dma, dma,
-            dma((5,)), dma((5,)), dma((4,)), dma((4,)), dma((3,)), dma((3,)),
+            dma((10,)), dma((D // COL,)), dma((2,)), dma((2,)), dma, dma, dma, dma,
+            dma((7,)), dma((7,)), dma((4,)), dma((4,)), dma((3,)), dma((3,)),
             dma((3, X)), dma((3, X)), dma((3, S)), dma((3, S)), dma((Z,)), dma((Z,)),
             pltpu.SemaphoreType.REGULAR, pltpu.SemaphoreType.REGULAR, pltpu.SemaphoreType.REGULAR,
         ],

time: 52.6 us -> 52.5 us (level)
  no operation moved by 1% of the time
where the time goes in v4:
time: 52.5 us; the launch traced here: 52.3 us
  Pallas kernels  51.7 us (98%)
  between operations  0.64 us (1%)
    pallas_call x1, Pallas kernels, per_device(): pl.pallas_call(functools.partial(kernel, norm), out_shape=(jax.ShapeDtype...  49.8 us
    pallas_call x1, Pallas kernels, per_device(): pl.pallas_call(deliver, out_shape=(jax.ShapeDtypeStruct(encoded.shape, BF...  1.87 us

profile of v4, /device:TPU:1, one launch (start us, length us, event | category | flops | bytes accessed | tf_op | source)
XLA Modules:
  0.0 52.3 jit_solution(8947649833103304467)
XLA Ops:
  0.6 49.8 %window_step.1 = (bf16[1,2,96,1536]{3,2,1,0:T(8,128)(2,1)}, f32[1,768]{1,0:T(1,128)}) custom-call(bf16[1,2,192,768]{3,2,1,0:T(8,128)(2,1)} %dna.1, bf16[3,768]{1,0:T(4,128)(2,1)} %dw.1, bf16[768,1536]{1,0:T(8,128)(2,1)} %pw.1, bf16[1536,512]{1,0:T(8,128)(2,1)} %qw.1, bf16[1536,128]{1,0:T(8,128)(2,1)} %kw.1, bf16[192,1536]{1,0:T(8,128)(2,1)} %bitcast.1, ...), custom_call_target="tpu_custom_call" | custom-call | tf_op jit(solution)/shard_map/window_step/pallas_call | solution.py:434
  50.5 1.9 %deliver.1 = (bf16[1,2,96,1536]{3,2,1,0:T(8,128)(2,1)}, f32[1,768]{1,0:T(1,128)}) custom-call(bf16[1,2,96,1536]{3,2,1,0:T(8,128)(2,1)} %get-tuple-element.4.encoded, f32[1,768]{1,0:T(1,128)} %get-tuple-element.5.grad), custom_call_target="tpu_custom_call" | custom-call | tf_op jit(solution)/shard_map/deliver/pallas_call | solution.py:483

commit v5 on v4

--- a/solution.py
+++ b/solution.py
@@ -138,8 +138,6 @@
         u = jnp.dot(pooled[...], pwv[:, cols], preferred_element_type=F32)
         enc[n] = gelu(u).astype(BF16).reshape(2, ROWS, COL)
 
-    pl.semaphore_wait(met1, 6)
-    signal(met2, [ahead, behind, z_peer(2), z_peer(Z - 2)])
     loads[6].wait()
     loads[7].wait()
     cot_copy = pltpu.make_async_remote_copy(
@@ -148,8 +146,8 @@
     )
     cot_copy.start()
 
-    to_left.wait()
-    to_right.wait()
+    to_left.wait_recv()
+    to_right.wait_recv()
     edge[...] = jnp.zeros_like(edge)
     for m in range(2):
         for k in range(6):
@@ -218,6 +216,8 @@
     to_near[0].start()
     to_near[1].start()
     to_near[2].start()
+    pl.semaphore_wait(met1, 6)
+    signal(met2, [ahead, behind, z_peer(2), z_peer(Z - 2)])
     rows, scale = project(g)
     relays = [relay(0, kvs.at[g])] + [relay(j, kvbuf.at[2 * j]) for j in range(1, 4)]
     relays[0].start()
@@ -235,8 +235,6 @@
     to_ahead.start()
     qall[:, 0] = q4[pl.ds(2 * c, 2)]
 
-    pl.semaphore_wait(met2, 4)
-    signal(met3, [sib, z_peer(2), z_peer(Z - 2)])
 
     def turn(k):
         wide = cotv[:, :, :, k * LANE : (k + 1) * LANE].astype(F32).reshape(4 * ROWS, LANE)
@@ -272,6 +270,8 @@
         weights = jnp.exp2(scores * EXP2_SCALE).astype(BF16)
         return jnp.dot(weights, value, preferred_element_type=F32)
 
+    pl.semaphore_wait(met2, 4)
+    signal(met3, [sib, z_peer(2), z_peer(Z - 2)])
     q_copy.wait_recv()
     relays[0].wait_recv()
     query = qall[...].reshape(4 * ROWS, KEY)
@@ -329,6 +329,7 @@
 
     for t in range(3):
         own[t] = share(t, True)
+        red1[t, Z * S :, :] = jnp.zeros((S * 16 - Z * S, LANE), F32)
     for t in range(3):
         att_copy(t).wait_recv()
         full = own[t] + share(t, False)
@@ -351,7 +352,6 @@
             p1_copy(t, d).wait_recv()
             total = total + p1r[t, d].astype(F32)
         red1[t, : Z * S, :] = total
-        red1[t, Z * S :, :] = jnp.zeros((S * 16 - Z * S, LANE), F32)
         for i in range(S):
             p2s[t, i] = red1[t, pl.ds(i, 16, stride=S), :].astype(BF16)
         for d in (4, 3, 5, 2, 6, 1, 7):
@@ -387,6 +387,8 @@
     grad_out[:, : 2 * VAL] = row[0]
     grad_out[:, 2 * VAL :] = row[1]
 
+    to_left.wait_send()
+    to_right.wait_send()
     cols = pl.ds(0, COL)
     for n in range(D // COL):
         pltpu.make_async_copy(enc.at[n], enc_out.at[0, :, :, cols], enc_sem.at[n]).wait()

time: 52.5 us -> 52.5 us (level)
  no operation moved by 1% of the time
where the time goes in v5:
time: 52.5 us; the launch traced here: 52.4 us
  Pallas kernels  51.8 us (99%)
  between operations  0.64 us (1%)
    pallas_call x1, Pallas kernels, per_device(): pl.pallas_call(functools.partial(kernel, norm), out_shape=(jax.ShapeDtype...  49.9 us
    pallas_call x1, Pallas kernels, per_device(): pl.pallas_call(deliver, out_shape=(jax.ShapeDtypeStruct(encoded.shape, BF...  1.87 us

profile of v5, /device:TPU:1, one launch (start us, length us, event | category | flops | bytes accessed | tf_op | source)
XLA Modules:
  0.0 52.4 jit_solution(774411276823707630)
XLA Ops:
  0.6 49.9 %window_step.1 = (bf16[1,2,96,1536]{3,2,1,0:T(8,128)(2,1)}, f32[1,768]{1,0:T(1,128)}) custom-call(bf16[1,2,192,768]{3,2,1,0:T(8,128)(2,1)} %dna.1, bf16[3,768]{1,0:T(4,128)(2,1)} %dw.1, bf16[768,1536]{1,0:T(8,128)(2,1)} %pw.1, bf16[1536,512]{1,0:T(8,128)(2,1)} %qw.1, bf16[1536,128]{1,0:T(8,128)(2,1)} %kw.1, bf16[192,1536]{1,0:T(8,128)(2,1)} %bitcast.1, ...), custom_call_target="tpu_custom_call" | custom-call | tf_op jit(solution)/shard_map/window_step/pallas_call | solution.py:436
  50.5 1.9 %deliver.1 = (bf16[1,2,96,1536]{3,2,1,0:T(8,128)(2,1)}, f32[1,768]{1,0:T(1,128)}) custom-call(bf16[1,2,96,1536]{3,2,1,0:T(8,128)(2,1)} %get-tuple-element.4.encoded, f32[1,768]{1,0:T(1,128)} %get-tuple-element.5.grad), custom_call_target="tpu_custom_call" | custom-call | tf_op jit(solution)/shard_map/deliver/pallas_call | solution.py:485
